TPU v7x, 512 devices: a whole 4x4x16 slice. The times are simulated.
512 devices in a mesh: fsdp: 128 (over y, z, core), tensor: 4 (over x).
Axes of the slice: x: 4, y: 4, z: 16, core: 2. Of those that a mesh axis runs over, the one named last changes fastest.
Arguments:
- gradients: bfloat16 [128, 1024, 1024], P(None, 'fsdp', 'tensor'), may hold values from -300 to 300
- parameters: bfloat16 [128, 1024, 1024], P(None, 'fsdp', 'tensor'), may hold values from -6 to 6
- left_root: bfloat16 [384, 1024, 1024], P('fsdp', 'tensor'), may hold values from -1 to 2
- right_root: bfloat16 [384, 1024, 1024], P('fsdp', None, 'tensor'), may hold values from -1 to 2
- assignment: int32 [128], replicated, may hold values from 0 to 383, as said below
Outputs:
- grafted_update: bfloat16 [128, 1024, 1024], P(None, 'fsdp', 'tensor')
- updated_params: bfloat16 [128, 1024, 1024], P(None, 'fsdp', 'tensor')
Inputs may be any that keep to these rules, and one draw needn't show every extreme that they name: `assignment`: distinct slot numbers; slot s belongs to owner s // 3. Every draw fills all 3 slots of some owner, which one is drawn; owner loads are skewed and about half the owners get none.
All inputs are finite; a program needn't handle non-finite values.
Results may differ from a plain program's by a relative error of at most 0.0049.
Values may be sent and summed in bfloat16 or wider, within the bound.
No kernel may reach another device: no remote copies, remote signals or barrier semaphores. Data moves between devices by JAX's collectives and lax.ppermute only.
A program may use at most 64 MiB of HBM per device.

v0:
```python
import jax
import jax.numpy as jnp
from jax import lax
from jax.sharding import PartitionSpec as P

graft_eps = 1e-06
step_rate = 0.1


def per_device(gradients, parameters, left_root, right_root, assignment):
    block_count, row_local, col_local = gradients.shape
    capacity = left_root.shape[0]
    block_width = right_root.shape[1]
    fsdp_size = lax.axis_size("fsdp")
    slot_total = fsdp_size * capacity
    block_ids = jnp.arange(block_count, dtype=jnp.int32)
    block_of = jnp.zeros((slot_total,), jnp.int32).at[assignment].set(block_ids)
    is_live = jnp.zeros((slot_total,), jnp.int32).at[assignment].set(1)
    pick_rows = block_of.reshape(fsdp_size, capacity).T
    used_slots = (is_live.reshape(fsdp_size, capacity).T > 0)[:, :, None, None]
    gathered = lax.all_gather(gradients, "tensor", axis=2, tiled=True)
    outgoing = jnp.where(used_slots, gathered[pick_rows], jnp.zeros((), gathered.dtype))
    arrived = lax.all_to_all(outgoing, "fsdp", split_axis=1, concat_axis=1, tiled=True)
    owned_blocks = arrived.reshape(capacity, block_width, block_width)
    left_mixed = jnp.einsum(
        "kij,kjc->kic", left_root, owned_blocks, preferred_element_type=jnp.float32
    ).astype(jnp.bfloat16)
    preconditioned = jnp.einsum(
        "kij,kjc->kic",
        lax.all_gather(left_mixed, "tensor", axis=1, tiled=True),
        right_root,
        preferred_element_type=jnp.float32,
    )
    update_part = jnp.sum(jnp.square(preconditioned), axis=(1, 2))
    grad_squares = jnp.sum(jnp.square(gradients.astype(jnp.float32)), axis=(1, 2))
    grad_block = lax.psum(grad_squares, ("fsdp", "tensor"))
    grad_by_slot = jnp.zeros((slot_total,), jnp.float32).at[assignment].set(grad_block)
    grad_total = lax.dynamic_slice_in_dim(
        grad_by_slot, lax.axis_index("fsdp") * capacity, capacity, 0
    )
    update_total = lax.psum(update_part, "tensor")
    entries = float(block_width * block_width)
    factor = jnp.sqrt(grad_total / entries + graft_eps) / jnp.sqrt(
        update_total / entries + graft_eps
    )
    update = (preconditioned * factor[:, None, None]).astype(jnp.bfloat16)
    returned = lax.all_to_all(
        update.reshape(capacity, fsdp_size, row_local, col_local),
        "fsdp",
        split_axis=1,
        concat_axis=1,
        tiled=True,
    )
    step_rows = returned[assignment % capacity, assignment // capacity]
    new_params = (
        parameters.astype(jnp.float32) - step_rate * step_rows.astype(jnp.float32)
    ).astype(jnp.bfloat16)
    return (step_rows, new_params)


def solution(mesh):
    return jax.shard_map(
        per_device,
        mesh=mesh,
        in_specs=(
            P(None, "fsdp", "tensor"),
            P(None, "fsdp", "tensor"),
            P("fsdp", "tensor", None),
            P("fsdp", None, "tensor"),
            P(),
        ),
        out_specs=(P(None, "fsdp", "tensor"), P(None, "fsdp", "tensor")),
        check_vma=False,
    )
```

profile of v0, /device:TPU:6, one launch (start us, length us, event | category | flops | bytes accessed | tf_op | source)
XLA Modules:
  0.0 581.2 jit_solution(4753571609893557137)
XLA Ops:
  7.2 0.7 all-gather.3.cloned.1.call-update
  8.0 0.7 fusion.18
  8.6 1.0 scatter_custom_fusion.1
  9.6 0.2 reshape.18
  9.9 1.0 scatter_custom_fusion
  10.9 0.2 gt.10
  11.3 44.8 %all-gather.3.cloned.1.call-done = bf16[128,8,1024]{2,1,0:T(8,128)(2,1)} async-done(((bf16[128,8,256]{2,1,0:T(8,128)(2,1)}), bf16[128,8,1024]{2,1,0:T(8,128)(2,1)}) %all-gather.3.cloned.1.call-update) | async-done | bytes 2097168 | tf_op jit(solution)/shard_map/all_gather | solution.py:21
  56.1 5.2 gather_fusion
  61.3 3.8 broadcast_select_fusion
  65.0 0.7 copy.16
  65.8 295.3 %all_to_all.10 = bf16[3,128,8,1024]{3,2,0,1:T(8,128)(2,1)S(1)} all-to-all(bf16[3,128,8,1024]{3,2,0,1:T(8,128)(2,1)S(1)} %copy.16), channel_id=1, replica_groups=mesh['fsdp'=128,'tensor'=4] {'fsdp'}, dimensions={1} | all-to-all | bytes 12582912 | tf_op jit(solution)/shard_map/all_to_all | solution.py:23
  361.1 3.4 fusion.7
  364.5 1.0 multiply_reduce_fusion.1
  365.6 99.6 %psum.14 = f32[128]{0:T(128)S(1)} all-reduce(f32[128]{0:T(128)S(1)} %multiply_reduce_fusion.1), channel_id=1, replica_groups=mesh['fsdp'=128,'tensor'=4] {'fsdp','tensor'}, use_global_device_ids=true, to_apply=%region_3.4 | all-reduce | flops 128 | bytes 1024 | tf_op jit(solution)/shard_map/psum | solution.py:36
  465.2 1.0 scatter_custom_fusion.2
  466.2 6.8 %multiply_reduce_fusion = (f32[3]{0:T(128)S(1)}, f32[3,1024,256]{2,1,0:T(8,128)}) fusion(bf16[3,1024,1024]{1,2,0:T(8,128)(2,1)} %all-gather.5.cloned.1.call-done, bf16[3,1024,256]{2,1,0:T(8,128)(2,1)S(1)} %copy-done), kind=kOutput, calls=%fused_computation.10 | convolution fusion | flops 1612185600 | bytes 11010060 | tf_op jit(solution)/shard_map/kij,kjc->kic/dot_general | solution.py:28
  473.0 8.6 %psum.15 = f32[3]{0:T(128)S(1)} all-reduce(f32[3]{0:T(128)S(1)} %get-tuple-element.4), channel_id=1, replica_groups=mesh['fsdp'=128,'tensor'=4] {'tensor'}, use_global_device_ids=true, to_apply=%region_6.7 | all-reduce | flops 3 | bytes 24 | tf_op jit(solution)/shard_map/psum | solution.py:41
  481.6 0.1 rsqrt_multiply_fusion
  481.7 2.2 fusion.6
  483.9 0.1 copy.20
  484.0 86.5 %all_to_all.11 = bf16[3,128,8,256]{3,2,0,1:T(8,128)(2,1)S(1)} all-to-all(bf16[3,128,8,256]{3,2,0,1:T(8,128)(2,1)S(1)} %copy.20), channel_id=1, replica_groups=mesh['fsdp'=128,'tensor'=4] {'fsdp'}, dimensions={1} | all-to-all | bytes 3145728 | tf_op jit(solution)/shard_map/all_to_all | solution.py:47
  570.5 0.1 copy.21
  570.6 1.6 gather_fusion.1
  572.3 2.2 subtract_convert_fusion
  (17 shorter events, 0.3 us)
Async XLA Ops:
  7.2 459.0 %copy-start = (bf16[3,1024,256]{2,1,0:T(8,128)(2,1)S(1)}, bf16[3,1024,256]{2,1,0:T(8,128)(2,1)}, u32[]{:S(2)}) copy-start(bf16[3,1024,256]{2,1,0:T(8,128)(2,1)} %param.8) | copy-start | bytes 4718596
  7.2 48.9 %all-gather.3.cloned.1.call-start = ((), (), s32[]{:S(2)}) async-start(), calls=%async_computation.2 | async-start | bytes 2621440 | tf_op jit(solution)/shard_map/all_gather | solution.py:21
  7.9 458.3 %all-gather.5.cloned.1.call-start = ((), (), s32[]{:S(2)}) async-start(), calls=%async_computation.3 | async-start | bytes 7864320 | tf_op jit(solution)/shard_map/all_gather | solution.py:30
  65.8 295.3 %copy-start.2 = (bf16[3,256,1024]{2,1,0:T(8,128)(2,1)S(1)}, bf16[3,256,1024]{2,1,0:T(8,128)(2,1)}, u32[]{:S(2)}) copy-start(bf16[3,256,1024]{2,1,0:T(8,128)(2,1)} %param.7) | copy-start | bytes 4718596
  361.0 3.5 copy-start.1
Sparse Core Ops, SparseCore 0:
  10.1 45.9 all-gather.2
  364.6 70.7 all-gather.4
where the time goes:
time: 584 us; the launch traced here: 581 us
  blocking collectives  490 us (84%)
  waiting for transfers between devices  45.5 us (8%)
  between operations  14.2 us (2%)
  local copies, waits for them, and re-layouts  11.3 us (2%)
  matrix products  10.2 us (2%)
  other arithmetic  9.94 us (2%)
    all_to_all x1, blocking collectives, per_device(): lax.all_to_all(outgoing, 'fsdp', split_axis=1, concat_axis=1, tiled=True)  295 us
    psum x1, blocking collectives, per_device(): grad_block = lax.psum(grad_squares, ('fsdp', 'tensor'))  99.6 us
    all_to_all x1, blocking collectives, per_device(): lax.all_to_all(update.reshape(capacity, fsdp_size, row_local, col_local),...  86.5 us
    all_gather x1, waiting for transfers between devices, per_device(): gathered = lax.all_gather(gradients, 'tensor', axis=2, tiled=True)  44.8 us
  transfers between devices with their start and end apart: 2, of which 1 were waited for; matrix products, arithmetic and copies ran while one was open for 1% of the time, Pallas kernels for 0%

commit v1 on v0

v1 whole, which is shorter than its diff:
```python
import functools
import jax
import jax.numpy as jnp
from jax import lax
from jax.experimental import pallas as pl
from jax.experimental.pallas import tpu as pltpu
from jax.sharding import Mesh, PartitionSpec as P

graft_eps = 1e-06
step_rate = 0.1

grid_y, grid_z, grid_core, grid_x = 4, 16, 2, 4
plane_axes = ("y", "core", "x")
fsdp_axes = ("y", "z", "core")
plane_devices = grid_y * grid_core * grid_x
plane_capacities = (13, 15, 16, 18, 24)

pick_run = 8


def pick_kernel(index_ref, src_ref, out_ref):
    def some(step, carry):
        first = step * pick_run
        rows = [src_ref[index_ref[first + i]] for i in range(pick_run)]
        for i in range(pick_run):
            out_ref[first + i] = rows[i]
        return carry

    lax.fori_loop(0, out_ref.shape[0] // pick_run, some, 0)


def pick_runs_kernel(strides, index_ref, src_ref, out_ref):
    src_run, src_step, out_run, out_step = strides

    def one(at, carry):
        src_at, out_at = index_ref[at] * src_run, at * out_run
        for z in range(grid_z):
            out_ref[out_at + z * out_step] = src_ref[src_at + z * src_step]
        return carry

    lax.fori_loop(0, index_ref.shape[0], one, 0)


def step_kernel(step_ref, parameter_ref, new_ref):
    def some(at, carry):
        rows = pl.ds(at * pick_run, pick_run)
        new_ref[rows] = (
            parameter_ref[rows].astype(jnp.float32)
            - step_rate * step_ref[rows].astype(jnp.float32)
        ).astype(new_ref.dtype)
        return carry

    lax.fori_loop(0, new_ref.shape[0] // pick_run, some, 0)


def vmem_call(kernel, index, arrays, count, name):
    vmem_spec = pl.BlockSpec(memory_space=pltpu.VMEM)
    index_specs = [pl.BlockSpec(memory_space=pltpu.SMEM)] * len(index)
    return pl.pallas_call(
        kernel,
        out_shape=jax.ShapeDtypeStruct((count,) + arrays[0].shape[1:], arrays[0].dtype),
        in_specs=index_specs + [vmem_spec] * len(arrays),
        out_specs=vmem_spec,
        compiler_params=pltpu.CompilerParams(vmem_limit_bytes=32 * 1024 * 1024),
        name=name,
    )(*index, *arrays)


def place(values, keys, size):
    hit = jnp.arange(size, dtype=jnp.int32)[:, None] == keys[None, :]
    return jnp.sum(jnp.where(hit, values[None, :], 0), axis=1)


def holder_x(slot, core):
    return (slot + 2 + core) % grid_x


def slot_at(x, core):
    return (x + 2 * grid_x - 2 - core) % grid_x


def factor_pieces(factor, here, core):
    slots = factor.shape[0]
    got = []
    for shift in range(1, grid_x):
        slot = jnp.minimum(slot_at(here + shift, core), slots - 1)
        piece = lax.dynamic_index_in_dim(factor, slot, 0, keepdims=False)
        pairs = [
            (at * grid_x + src, at * grid_x + (src + shift) % grid_x)
            for at in range(grid_core)
            for src in range(grid_x)
            if slot_at((src + shift) % grid_x, at) < slots
        ]
        got.append(lax.ppermute(piece, ("core", "x"), pairs))
    return got


def slot_kernel(here_ref, *refs):
    rows = refs[0]
    lefts = refs[1 : 1 + grid_x]
    rights = refs[1 + grid_x : 1 + 2 * grid_x]
    out, left, right, block, mixed, product, sems = refs[1 + 2 * grid_x :]
    here, slot = here_ref[0], here_ref[1]
    order = block.shape[0]
    share = order // grid_x
    row_local = rows.shape[2]
    pair = grid_core * row_local
    tiles = order // pair
    copies = []
    for shift in range(grid_x):
        at = lax.rem(here - shift + grid_x, grid_x)
        left_src = lefts[0].at[slot] if shift == 0 else lefts[shift]
        right_src = rights[0].at[slot] if shift == 0 else rights[shift]
        copies.append(
            (
                pltpu.make_async_copy(left_src, left.at[at], sems.at[shift]),
                pltpu.make_async_copy(right_src, right.at[at], sems.at[grid_x + shift]),
            )
        )
    for copy, unused in copies:
        copy.start()
    for unused, copy in copies:
        copy.start()

    def gather_tile(tile, total):
        y, z = tile // grid_z, tile % grid_z
        at = pl.ds(pl.multiple_of(tile * pair, pair), pair)
        for x in range(grid_x):
            both = jnp.concatenate(
                [
                    rows[(y * grid_core + core) * grid_x + x, z].astype(jnp.float32)
                    for core in range(grid_core)
                ],
                axis=0,
            )
            total = total + both * both
            block[at, x * share : (x + 1) * share] = both.astype(block.dtype)
        return total

    grad_sum = lax.fori_loop(
        0, tiles, gather_tile, jnp.zeros((pair, share), jnp.float32)
    )
    for copy, unused in copies:
        copy.wait()

    def mix(tile, carry):
        at = pl.ds(pl.multiple_of(tile * share, share), share)
        for x in range(grid_x):
            mixed[x * share : (x + 1) * share, at] = jnp.dot(
                left[x], block[:, at], preferred_element_type=jnp.float32
            ).astype(mixed.dtype)
        return carry

    lax.fori_loop(0, grid_x, mix, 0)
    for unused, copy in copies:
        copy.wait()

    def finish(x, total):
        for tile in range(grid_x):
            at = slice(tile * share, (tile + 1) * share)
            part = jnp.dot(mixed[at, :], right[x], preferred_element_type=jnp.float32)
            product[x, at] = part
            total = total + jnp.sum(jnp.square(part), axis=0, keepdims=True)
        return total

    update_sum = lax.fori_loop(0, grid_x, finish, jnp.zeros((1, share), jnp.float32))
    entries = float(order * order)
    grad_ms = jnp.sum(grad_sum, axis=(0, 1), keepdims=True) / entries
    update_ms = jnp.sum(update_sum, axis=(0, 1), keepdims=True) / entries
    factor = jnp.sqrt(grad_ms + graft_eps) / jnp.sqrt(update_ms + graft_eps)

    def scatter_tile(tile, carry):
        y, z = tile // grid_z, tile % grid_z
        at = pl.ds(pl.multiple_of(tile * pair, pair), pair)
        for x in range(grid_x):
            scaled = (product[x, at, :] * factor).reshape(grid_core, row_local, share)
            for core in range(grid_core):
                out[(y * grid_core + core) * grid_x + x, z] = scaled[core].astype(out.dtype)
        return carry

    lax.fori_loop(0, tiles, scatter_tile, 0)


def precondition_slot(here, core, rows, left_root, right_root, left_pieces, right_pieces):
    slots, order = right_root.shape[:2]
    share = order // grid_x
    any_spec = pl.BlockSpec(memory_space=pl.ANY)
    vmem_spec = pl.BlockSpec(memory_space=pltpu.VMEM)
    return pl.pallas_call(
        slot_kernel,
        out_shape=jax.ShapeDtypeStruct(rows.shape, rows.dtype),
        in_specs=[pl.BlockSpec(memory_space=pltpu.SMEM)]
        + [vmem_spec]
        + [any_spec] * (2 * grid_x),
        out_specs=vmem_spec,
        scratch_shapes=[
            pltpu.VMEM((grid_x, share, order), jnp.bfloat16),
            pltpu.VMEM((grid_x, order, share), jnp.bfloat16),
            pltpu.VMEM((order, order), jnp.bfloat16),
            pltpu.VMEM((order, order), jnp.bfloat16),
            pltpu.VMEM((grid_x, order, share), jnp.float32),
            pltpu.SemaphoreType.DMA((2 * grid_x,)),
        ],
        compiler_params=pltpu.CompilerParams(vmem_limit_bytes=40 * 1024 * 1024),
        cost_estimate=pl.CostEstimate(
            flops=4 * order**3, bytes_accessed=8 * order * order, transcendentals=0
        ),
        name="precondition_slot",
    )(
        jnp.stack([here, jnp.minimum(slot_at(here, core), slots - 1)]),
        rows,
        left_root,
        *left_pieces,
        right_root,
        *right_pieces,
    )


def program(plane_cap, gradients, parameters, left_root, right_root, assignment):
    block_count, row_local, col_local = gradients.shape
    slots_each = left_root.shape[0]
    chunk = (row_local, col_local)
    here, core = lax.axis_index("x"), lax.axis_index("core")
    left_pieces = factor_pieces(left_root, here, core)
    right_pieces = factor_pieces(right_root, here, core)

    owner = assignment // slots_each
    plane = (owner // grid_core) % grid_z
    owner_core = owner % grid_core
    in_plane = ((owner // (grid_z * grid_core)) * grid_core + owner_core) * grid_x + holder_x(
        assignment % slots_each, owner_core
    )
    ids = jnp.arange(block_count, dtype=jnp.int32)
    earlier = (plane[:, None] == plane[None, :]) & (ids[None, :] < ids[:, None])
    rank = jnp.sum(earlier.astype(jnp.int32), axis=1)
    place_of = plane * plane_cap + rank
    my_z = lax.axis_index("z")
    block_at = place(ids, place_of, grid_z * plane_cap)
    mine = plane == my_z
    rank_at = place(rank, jnp.where(mine, in_plane, plane_devices), plane_devices)
    holder_at = place(in_plane, jnp.where(mine, rank, plane_cap), plane_cap)
    plane_rows, z_rows = plane_devices * grid_z, grid_z * plane_cap

    def z_hop(rows):
        rows = rows.reshape((grid_z, plane_cap) + chunk)
        return lax.all_to_all(rows, "z", 0, 0, tiled=True).reshape((z_rows,) + chunk)

    def plane_hop(rows):
        rows = rows.reshape((plane_devices, grid_z) + chunk)
        return lax.all_to_all(rows, plane_axes, 0, 0, tiled=True)

    rows = vmem_call(pick_kernel, [block_at], [gradients], z_rows, "pick_for_z")
    rows, left_pieces, right_pieces = lax.optimization_barrier(
        (z_hop(rows), left_pieces, right_pieces)
    )
    kernel = functools.partial(pick_runs_kernel, (1, plane_cap, grid_z, 1))
    rows = vmem_call(kernel, [rank_at], [rows], plane_rows, "pick_for_plane")
    rows = plane_hop(rows)
    update = precondition_slot(
        here, core, rows, left_root, right_root, left_pieces, right_pieces
    )
    update = plane_hop(update).reshape((plane_rows,) + chunk)
    kernel = functools.partial(pick_runs_kernel, (grid_z, 1, 1, plane_cap))
    update = vmem_call(kernel, [holder_at], [update], z_rows, "pick_back_for_z")
    update = z_hop(update)
    step_rows = vmem_call(pick_kernel, [place_of], [update], block_count, "pick_step_rows")
    new_params = vmem_call(step_kernel, [], [step_rows, parameters], block_count, "step")
    return step_rows, new_params


def per_device(gradients, parameters, left_root, right_root, assignment):
    plane = (assignment // (left_root.shape[0] * grid_core)) % grid_z
    loads = jnp.sum(
        (plane[None, :] == jnp.arange(grid_z, dtype=jnp.int32)[:, None]).astype(jnp.int32), axis=1
    )
    caps = jnp.array(plane_capacities[:-1], jnp.int32)
    choice = jnp.max(jnp.sum((loads[:, None] > caps[None, :]).astype(jnp.int32), axis=1))
    branches = [functools.partial(program, cap) for cap in plane_capacities]
    return lax.switch(choice, branches, gradients, parameters, left_root, right_root, assignment)


def solution(mesh):
    grid = Mesh(
        mesh.devices.reshape(grid_y, grid_z, grid_core, grid_x), ("y", "z", "core", "x")
    )
    return jax.shard_map(
        per_device,
        mesh=grid,
        in_specs=(
            P(None, fsdp_axes, "x"),
            P(None, fsdp_axes, "x"),
            P(fsdp_axes, "x", None),
            P(fsdp_axes, None, "x"),
            P(),
        ),
        out_specs=(P(None, fsdp_axes, "x"), P(None, fsdp_axes, "x")),
        check_vma=False,
    )
```

time: 584 us -> 235 us (0.40)
  blocking collectives: 490 us -> 71 us
  starting transfers between devices: 0.08 us -> 44.1 us
  waiting for transfers between devices: 45.5 us -> 86.1 us
  Pallas kernels: 0 us -> 15.9 us
  between operations: 14.2 us -> 1.28 us
  matrix products: 10.2 us -> 0 us
  other arithmetic: 9.94 us -> 3.48 us
    all_to_all x2 -> x1, blocking collectives: 382 us -> 71 us  [z_hop(): lax.all_to_all(rows, 'z', 0, 0, tiled=True).reshape((z_rows,) + chunk)]
    psum x2 -> x0, blocking collectives: 108 us -> none  [the longest x1 99.6 us: per_device(): grad_block = lax.psum(grad_squares, ('fsdp', 'tensor'))]
    all_to_all x0 -> x3, waiting for transfers between devices: none -> 51.5 us  [the longest x2 51.5 us: plane_hop(): return lax.all_to_all(rows, plane_axes, 0, 0, tiled=True)]
    all_gather x2 -> x0, waiting for transfers between devices: 44.8 us -> none  [the longest x1 44.8 us: per_device(): gathered = lax.all_gather(gradients, 'tensor', axis=2, tiled=True)]
    ppermute x0 -> x6, waiting for transfers between devices: none -> 34.6 us  [factor_pieces(): got.append(lax.ppermute(piece, ('core', 'x'), pairs))]
    all_to_all x0 -> x3, starting transfers between devices: none -> 29.2 us  [the longest x1 15.2 us: z_hop(): lax.all_to_all(rows, 'z', 0, 0, tiled=True).reshape((z_rows,) + chunk)]
    pallas_call x0 -> x6, Pallas kernels: none -> 15.9 us  [the longest x1 8.67 us: precondition_slot(): pl.pallas_call(slot_kernel, out_shape=jax.ShapeDtypeStruct(rows.shape, ro...]
    ppermute x0 -> x6, starting transfers between devices: none -> 14.9 us  [factor_pieces(): got.append(lax.ppermute(piece, ('core', 'x'), pairs))]
  transfers between devices with their start and end apart: 2 -> 9, of which waited for: 1 -> 6; matrix products, arithmetic and copies ran while one was open for 1% -> 1% of each run, Pallas kernels for 0% -> 0%
where the time goes in v1:
time: 235 us; the launch traced here: 233 us
  waiting for transfers between devices  86.1 us (37%)
  blocking collectives  71 us (30%)
  starting transfers between devices  44.1 us (19%)
  Pallas kernels  15.9 us (7%)
  local copies, waits for them, and re-layouts  10.8 us (5%)
  other arithmetic  3.48 us (1%)
    all_to_all x1, blocking collectives, z_hop(): lax.all_to_all(rows, 'z', 0, 0, tiled=True).reshape((z_rows,) + chunk)  71 us
    all_to_all x2, waiting for transfers between devices, plane_hop(): return lax.all_to_all(rows, plane_axes, 0, 0, tiled=True)  51.5 us
    ppermute x6, waiting for transfers between devices, factor_pieces(): got.append(lax.ppermute(piece, ('core', 'x'), pairs))  34.6 us
    all_to_all x1, starting transfers between devices, z_hop(): lax.all_to_all(rows, 'z', 0, 0, tiled=True).reshape((z_rows,) + chunk)  15.2 us
    ppermute x6, starting transfers between devices, factor_pieces(): got.append(lax.ppermute(piece, ('core', 'x'), pairs))  14.9 us
    all_to_all x2, starting transfers between devices, plane_hop(): return lax.all_to_all(rows, plane_axes, 0, 0, tiled=True)  14 us
    pallas_call x1, Pallas kernels, precondition_slot(): pl.pallas_call(slot_kernel, out_shape=jax.ShapeDtypeStruct(rows.shape, ro...  8.67 us
    cond x22, local copies, waits for them, and re-layouts  7.87 us
  transfers between devices with their start and end apart: 9, of which 6 were waited for; matrix products, arithmetic and copies ran while one was open for 1% of the time, Pallas kernels for 0%

profile of v1, /device:TPU:6, one launch (start us, length us, event | category | flops | bytes accessed | tf_op | source)
XLA Modules:
  0.0 233.2 jit_solution(14889768485886329231)
XLA Ops:
  3.5 229.8 %conditional.1 = (bf16[128,8,256]{2,1,0:T(8,128)(2,1)}, bf16[128,8,256]{2,1,0:T(8,128)(2,1)}) conditional(s32[]{:T(128)} %clamp.3, (s32[128]{0:T(128)}, bf16[128,8,256]{2,1,0:T(8,128)(2,1)}, bf16[3,256,1024]{2,1,0:T(8,128)(2,1)}, bf16[3,1024,256]{2,1,0:T(8,128)(2,1)}, bf16[128,8,256]{2,1,0:T(8,128)(2,1)}) %tuple.32, ...), branch_computations={%region_3.8_spmd, %region_8.13_spmd, %region_13.18_spmd, %region_1... | conditional | flops 4295227392 | bytes 77081256 | solution.py:279
  4.7 2.6 %pick_for_z.8 = bf16[288,8,256]{2,1,0:T(8,128)(2,1)} custom-call(s32[288]{0:T(512)S(1)} %select_reduce_fusion.9.index_ref, bf16[128,8,256]{2,1,0:T(8,128)(2,1)} %get-tuple-element.87.src_ref), custom_call_target="tpu_custom_call" | custom-call | tf_op jit(solution)/shard_map/cond/branch_3_fun/pick_for_z/pallas_call | solution.py:59
  7.3 15.2 %all-to-all-start.12 = ((bf16[16,18,8,256]{3,2,1,0:T(8,128)(2,1)}), bf16[16,18,8,256]{3,2,1,0:T(8,128)(2,1)S(1)}, u32[]{:S(2)}, u32[]{:S(2)}) async-start(bf16[16,18,8,256]{3,2,1,0:T(8,128)(2,1)} %bitcast.44), calls=%async_computation.12 | async-start | bytes 2359296 | tf_op jit(solution)/shard_map/cond/branch_3_fun/all_to_all | solution.py:246
  22.6 1.5 dynamic-slice_bitcast_fusion.21
  24.1 2.7 %collective-permute-start.20 = (bf16[256,1024]{1,0:T(8,128)(2,1)S(1)}, bf16[256,1024]{1,0:T(8,128)(2,1)S(1)}, u32[]{:S(2)}, u32[]{:S(2)}) collective-permute-start(bf16[256,1024]{1,0:T(8,128)(2,1)S(1)} %get-tuple-element.155), channel_id=1, source_target_pairs={{0,3},{1,0},{3,2},{4,7},{5,4},{6,5},{8,11},{9,8},{11,10},{12,15},{... | collective-permute-start | bytes 1572872 | tf_op jit(solution)/shard_map/cond/branch_3_fun/ppermute | solution.py:94
  26.8 1.3 collective-permute-start.19
  28.1 4.9 %collective-permute-start.18 = (bf16[256,1024]{1,0:T(8,128)(2,1)S(1)}, bf16[256,1024]{1,0:T(8,128)(2,1)S(1)}, u32[]{:S(2)}, u32[]{:S(2)}) collective-permute-start(bf16[256,1024]{1,0:T(8,128)(2,1)S(1)} %get-tuple-element.157), channel_id=1, source_target_pairs={{1,2},{2,3},{3,0},{4,5},{6,7},{7,4},{9,10},{10,11},{11,8},{12,13},... | collective-permute-start | bytes 1572872 | tf_op jit(solution)/shard_map/cond/branch_3_fun/ppermute | solution.py:94
  33.1 1.5 dynamic-slice_bitcast_fusion.18
  34.5 2.8 %collective-permute-start.23 = (bf16[1024,256]{1,0:T(8,128)(2,1)S(1)}, bf16[1024,256]{1,0:T(8,128)(2,1)S(1)}, u32[]{:S(2)}, u32[]{:S(2)}) collective-permute-start(bf16[1024,256]{1,0:T(8,128)(2,1)S(1)} %get-tuple-element.152), channel_id=1, source_target_pairs={{0,3},{1,0},{3,2},{4,7},{5,4},{6,5},{8,11},{9,8},{11,10},{12,15},{... | collective-permute-start | bytes 1572872 | tf_op jit(solution)/shard_map/cond/branch_3_fun/ppermute | solution.py:94
  37.3 1.3 collective-permute-start.22
  38.6 14.6 %collective-permute-done.20.refs_4_ = bf16[256,1024]{1,0:T(8,128)(2,1)S(1)} collective-permute-done((bf16[256,1024]{1,0:T(8,128)(2,1)S(1)}, bf16[256,1024]{1,0:T(8,128)(2,1)S(1)}, u32[]{:S(2)}, u32[]{:S(2)}) %collective-permute-start.20) | collective-permute-done | bytes 524320 | tf_op jit(solution)/shard_map/cond/branch_3_fun/ppermute | solution.py:94
  53.3 1.9 collective-permute-start.21
  56.1 18.2 %collective-permute-done.23.refs_8_ = bf16[1024,256]{1,0:T(8,128)(2,1)S(1)} collective-permute-done((bf16[1024,256]{1,0:T(8,128)(2,1)S(1)}, bf16[1024,256]{1,0:T(8,128)(2,1)S(1)}, u32[]{:S(2)}, u32[]{:S(2)}) %collective-permute-start.23) | collective-permute-done | bytes 524320 | tf_op jit(solution)/shard_map/cond/branch_3_fun/ppermute | solution.py:94
  77.6 2.2 pick_for_plane.8
  79.8 7.5 %all-to-all-start.13 = ((bf16[32,16,8,256]{3,2,1,0:T(8,128)(2,1)}), bf16[32,16,8,256]{3,2,1,0:T(8,128)(2,1)S(1)}, u32[]{:S(2)}, u32[]{:S(2)}) async-start(bf16[32,16,8,256]{3,2,1,0:T(8,128)(2,1)} %bitcast.52), calls=%async_computation.13 | async-start | bytes 4194304 | tf_op jit(solution)/shard_map/cond/branch_3_fun/all_to_all | solution.py:250
  87.4 25.7 %all-to-all-done.13.refs_0_ = bf16[32,16,8,256]{3,2,1,0:T(8,128)(2,1)S(1)} async-done(((bf16[32,16,8,256]{3,2,1,0:T(8,128)(2,1)}), bf16[32,16,8,256]{3,2,1,0:T(8,128)(2,1)S(1)}, u32[]{:S(2)}, u32[]{:S(2)}) %all-to-all-start.13) | async-done | bytes 2097184 | tf_op jit(solution)/shard_map/cond/branch_3_fun/all_to_all | solution.py:250
  113.1 1.0 copy-done.12
  115.2 1.0 copy-done.32
  116.2 1.0 copy-done.42
  117.3 8.7 %precondition_slot.8 = bf16[32,16,8,256]{3,2,1,0:T(8,128)(2,1)S(1)} custom-call(s32[2]{0:T(128)S(1)} %pad_add_fusion.3.here_ref, bf16[32,16,8,256]{3,2,1,0:T(8,128)(2,1)S(1)} %all-to-all-done.13.refs_0_, bf16[3,256,1024]{2,1,0:T(8,128)(2,1)} %get-tuple-element.88.refs_1_, bf16[256,1024]{1,0:T(8,128)(2,1)S(1)} %copy-done.12, ...), custom_call_target="tpu_custom_call" | custom-call | flops 4294967296 | bytes 8388608 | tf_op jit(solution)/shard_map/cond/branch_3_fun/precondition_slot/pallas_call | solution.py:189
  126.0 1.3 copy-done.3
  127.3 6.5 %all-to-all-start.14 = ((bf16[32,16,8,256]{3,2,1,0:T(8,128)(2,1)}), bf16[32,16,8,256]{3,2,1,0:T(8,128)(2,1)S(1)}, u32[]{:S(2)}, u32[]{:S(2)}) async-start(bf16[32,16,8,256]{3,2,1,0:T(8,128)(2,1)} %copy-done.3), calls=%async_computation.14 | async-start | bytes 4194304 | tf_op jit(solution)/shard_map/cond/branch_3_fun/all_to_all | solution.py:250
  133.9 25.7 %all-to-all-done.14 = bf16[32,16,8,256]{3,2,1,0:T(8,128)(2,1)S(1)} async-done(((bf16[32,16,8,256]{3,2,1,0:T(8,128)(2,1)}), bf16[32,16,8,256]{3,2,1,0:T(8,128)(2,1)S(1)}, u32[]{:S(2)}, u32[]{:S(2)}) %all-to-all-start.14) | async-done | bytes 2097184 | tf_op jit(solution)/shard_map/cond/branch_3_fun/all_to_all | solution.py:250
  160.4 71.0 %all_to_all.83 = bf16[16,18,8,256]{3,2,1,0:T(8,128)(2,1)S(1)} all-to-all(bf16[16,18,8,256]{3,2,1,0:T(8,128)(2,1)S(1)} %bitcast.109), channel_id=1, replica_groups=mesh['y'=4,'z'=16,'core'=2,'x'=4] {'z'}, dimensions={0} | all-to-all | bytes 2359296 | tf_op jit(solution)/shard_map/cond/branch_3_fun/all_to_all | solution.py:246
  (37 shorter events, 11.2 us)
Async XLA Ops:
  7.3 70.3 %all-to-all-start.12 = ((bf16[16,18,8,256]{3,2,1,0:T(8,128)(2,1)}), bf16[16,18,8,256]{3,2,1,0:T(8,128)(2,1)S(1)}, u32[]{:S(2)}, u32[]{:S(2)}) async-start(bf16[16,18,8,256]{3,2,1,0:T(8,128)(2,1)} %bitcast.44), calls=%async_computation.12 | async-start | bytes 2359296 | tf_op jit(solution)/shard_map/cond/branch_3_fun/all_to_all | solution.py:246
  24.1 29.2 %collective-permute-start.20 = (bf16[256,1024]{1,0:T(8,128)(2,1)S(1)}, bf16[256,1024]{1,0:T(8,128)(2,1)S(1)}, u32[]{:S(2)}, u32[]{:S(2)}) collective-permute-start(bf16[256,1024]{1,0:T(8,128)(2,1)S(1)} %get-tuple-element.155), channel_id=1, source_target_pairs={{0,3},{1,0},{3,2},{4,7},{5,4},{6,5},{8,11},{9,8},{11,10},{12,15},{... | collective-permute-start | bytes 1572872 | tf_op jit(solution)/shard_map/cond/branch_3_fun/ppermute | solution.py:94
  26.8 28.5 %collective-permute-start.19 = (bf16[256,1024]{1,0:T(8,128)(2,1)S(1)}, bf16[256,1024]{1,0:T(8,128)(2,1)S(1)}, u32[]{:S(2)}, u32[]{:S(2)}) collective-permute-start(bf16[256,1024]{1,0:T(8,128)(2,1)S(1)} %get-tuple-element.156), channel_id=1, source_target_pairs={{0,2},{1,3},{2,0},{5,7},{6,4},{7,5},{8,10},{9,11},{10,8},{13,15},{... | collective-permute-start | bytes 1572872 | tf_op jit(solution)/shard_map/cond/branch_3_fun/ppermute | solution.py:94
  28.1 28.0 %collective-permute-start.18 = (bf16[256,1024]{1,0:T(8,128)(2,1)S(1)}, bf16[256,1024]{1,0:T(8,128)(2,1)S(1)}, u32[]{:S(2)}, u32[]{:S(2)}) collective-permute-start(bf16[256,1024]{1,0:T(8,128)(2,1)S(1)} %get-tuple-element.157), channel_id=1, source_target_pairs={{1,2},{2,3},{3,0},{4,5},{6,7},{7,4},{9,10},{10,11},{11,8},{12,13},... | collective-permute-start | bytes 1572872 | tf_op jit(solution)/shard_map/cond/branch_3_fun/ppermute | solution.py:94
  34.5 39.7 %collective-permute-start.23 = (bf16[1024,256]{1,0:T(8,128)(2,1)S(1)}, bf16[1024,256]{1,0:T(8,128)(2,1)S(1)}, u32[]{:S(2)}, u32[]{:S(2)}) collective-permute-start(bf16[1024,256]{1,0:T(8,128)(2,1)S(1)} %get-tuple-element.152), channel_id=1, source_target_pairs={{0,3},{1,0},{3,2},{4,7},{5,4},{6,5},{8,11},{9,8},{11,10},{12,15},{... | collective-permute-start | bytes 1572872 | tf_op jit(solution)/shard_map/cond/branch_3_fun/ppermute | solution.py:94
  37.3 37.7 %collective-permute-start.22 = (bf16[1024,256]{1,0:T(8,128)(2,1)S(1)}, bf16[1024,256]{1,0:T(8,128)(2,1)S(1)}, u32[]{:S(2)}, u32[]{:S(2)}) collective-permute-start(bf16[1024,256]{1,0:T(8,128)(2,1)S(1)} %get-tuple-element.153), channel_id=1, source_target_pairs={{0,2},{1,3},{2,0},{5,7},{6,4},{7,5},{8,10},{9,11},{10,8},{13,15},{... | collective-permute-start | bytes 1572872 | tf_op jit(solution)/shard_map/cond/branch_3_fun/ppermute | solution.py:94
  53.3 23.6 %collective-permute-start.21 = (bf16[1024,256]{1,0:T(8,128)(2,1)S(1)}, bf16[1024,256]{1,0:T(8,128)(2,1)S(1)}, u32[]{:S(2)}, u32[]{:S(2)}) collective-permute-start(bf16[1024,256]{1,0:T(8,128)(2,1)S(1)} %get-tuple-element.154), channel_id=1, source_target_pairs={{1,2},{2,3},{3,0},{4,5},{6,7},{7,4},{9,10},{10,11},{11,8},{12,13},... | collective-permute-start | bytes 1572872 | tf_op jit(solution)/shard_map/cond/branch_3_fun/ppermute | solution.py:94
  56.1 23.7 %copy-start.11 = (bf16[256,1024]{1,0:T(8,128)(2,1)}, bf16[256,1024]{1,0:T(8,128)(2,1)S(1)}, u32[]{:S(2)}) copy-start(bf16[256,1024]{1,0:T(8,128)(2,1)S(1)} %collective-permute-done.18.refs_2_) | copy-start | bytes 1572868 | tf_op jit(solution)/shard_map/cond
  74.3 0.8 copy-start.21
  75.1 0.8 copy-start.31
  76.8 0.8 copy-start.41
  79.8 33.3 %all-to-all-start.13 = ((bf16[32,16,8,256]{3,2,1,0:T(8,128)(2,1)}), bf16[32,16,8,256]{3,2,1,0:T(8,128)(2,1)S(1)}, u32[]{:S(2)}, u32[]{:S(2)}) async-start(bf16[32,16,8,256]{3,2,1,0:T(8,128)(2,1)} %bitcast.52), calls=%async_computation.13 | async-start | bytes 4194304 | tf_op jit(solution)/shard_map/cond/branch_3_fun/all_to_all | solution.py:250
  113.1 1.0 copy-start.12
  114.2 1.0 copy-start.22
  115.2 1.0 copy-start.32
  116.2 1.0 copy-start.42
  126.0 1.3 copy-start.3
  127.3 32.4 %all-to-all-start.14 = ((bf16[32,16,8,256]{3,2,1,0:T(8,128)(2,1)}), bf16[32,16,8,256]{3,2,1,0:T(8,128)(2,1)S(1)}, u32[]{:S(2)}, u32[]{:S(2)}) async-start(bf16[32,16,8,256]{3,2,1,0:T(8,128)(2,1)} %copy-done.3), calls=%async_computation.14 | async-start | bytes 4194304 | tf_op jit(solution)/shard_map/cond/branch_3_fun/all_to_all | solution.py:250
  160.4 71.8 %copy-start.53 = (bf16[128,8,256]{2,1,0:T(8,128)(2,1)S(1)}, bf16[128,8,256]{2,1,0:T(8,128)(2,1)}, u32[]{:S(2)}) copy-start(bf16[128,8,256]{2,1,0:T(8,128)(2,1)} %get-tuple-element.97.parameter_ref) | copy-start | bytes 1572868 | tf_op jit(solution)/shard_map/cond
  232.2 1.1 copy-start.48

commit v2 on v1

--- a/solution.py
+++ b/solution.py
@@ -79,12 +79,45 @@
     return (x + 2 * grid_x - 2 - core) % grid_x
 
 
-def factor_pieces(factor, here, core):
-    slots = factor.shape[0]
+def pack_kernel(slot_ref, left_ref, right_ref, *refs):
+    sems, share = refs[-1], left_ref.shape[1]
+    copies = []
+    for at, out in enumerate(refs[:-1]):
+        slot = slot_ref[at]
+        copies.append(
+            pltpu.make_async_copy(left_ref.at[slot], out.at[:share], sems.at[at * (grid_x + 1)])
+        )
+        for part in range(grid_x):
+            span = pl.ds(part * share, share)
+            copies.append(
+                pltpu.make_async_copy(
+                    right_ref.at[slot, span],
+                    out.at[share:, span],
+                    sems.at[at * (grid_x + 1) + 1 + part],
+                )
+            )
+    for copy in copies:
+        copy.start()
+    for copy in copies:
+        copy.wait()
+
+
+def factor_pieces(left_root, right_root, here, core):
+    slots, share, order = left_root.shape
+    shifts = range(1, grid_x)
+    wanted = jnp.stack([jnp.minimum(slot_at(here + shift, core), slots - 1) for shift in shifts])
+    hbm_spec = pl.BlockSpec(memory_space=pltpu.HBM)
+    packed = pl.pallas_call(
+        pack_kernel,
+        out_shape=[jax.ShapeDtypeStruct((2 * share, order), left_root.dtype) for shift in shifts],
+        in_specs=[pl.BlockSpec(memory_space=pltpu.SMEM), hbm_spec, hbm_spec],
+        out_specs=[pl.BlockSpec(memory_space=pltpu.VMEM)] * len(shifts),
+        scratch_shapes=[pltpu.SemaphoreType.DMA((len(shifts) * (grid_x + 1),))],
+        compiler_params=pltpu.CompilerParams(vmem_limit_bytes=32 * 1024 * 1024),
+        name="pack_factors",
+    )(wanted, left_root, right_root)
     got = []
-    for shift in range(1, grid_x):
-        slot = jnp.minimum(slot_at(here + shift, core), slots - 1)
-        piece = lax.dynamic_index_in_dim(factor, slot, 0, keepdims=False)
+    for shift, piece in zip(shifts, packed):
         pairs = [
             (at * grid_x + src, at * grid_x + (src + shift) % grid_x)
             for at in range(grid_core)
@@ -95,31 +128,41 @@
     return got
 
 
+last_sem = 2 + (grid_x - 1) * (grid_x + 1)
+
+
 def slot_kernel(here_ref, *refs):
-    rows = refs[0]
-    lefts = refs[1 : 1 + grid_x]
-    rights = refs[1 + grid_x : 1 + 2 * grid_x]
-    out, left, right, block, mixed, product, sems = refs[1 + 2 * grid_x :]
+    arrived, own_left, own_right = refs[:3]
+    pieces = refs[3 : 2 + grid_x]
+    out, left, right, rows, block, mixed, product, staged, sems = refs[2 + grid_x :]
     here, slot = here_ref[0], here_ref[1]
     order = block.shape[0]
     share = order // grid_x
     row_local = rows.shape[2]
     pair = grid_core * row_local
     tiles = order // pair
-    copies = []
-    for shift in range(grid_x):
+    left_copies = [pltpu.make_async_copy(own_left.at[slot], left.at[here], sems.at[0])]
+    right_copies = [pltpu.make_async_copy(own_right.at[slot], right.at[here], sems.at[1])]
+    for piece in pieces:
+        shift = len(left_copies)
         at = lax.rem(here - shift + grid_x, grid_x)
-        left_src = lefts[0].at[slot] if shift == 0 else lefts[shift]
-        right_src = rights[0].at[slot] if shift == 0 else rights[shift]
-        copies.append(
-            (
-                pltpu.make_async_copy(left_src, left.at[at], sems.at[shift]),
-                pltpu.make_async_copy(right_src, right.at[at], sems.at[grid_x + shift]),
+        first = 2 + (shift - 1) * (grid_x + 1)
+        left_copies.append(
+            pltpu.make_async_copy(piece.at[:share], left.at[at], sems.at[first])
+        )
+        for part in range(grid_x):
+            span = pl.ds(part * share, share)
+            right_copies.append(
+                pltpu.make_async_copy(
+                    piece.at[share:, span], right.at[at, span], sems.at[first + 1 + part]
+                )
             )
-        )
-    for copy, unused in copies:
-        copy.start()
-    for unused, copy in copies:
+    spans = [pl.ds(y * grid_core * grid_x, grid_core * grid_x) for y in range(grid_y)]
+    row_copies = [
+        pltpu.make_async_copy(arrived.at[span], rows.at[span], sems.at[last_sem + grid_y + y])
+        for y, span in enumerate(spans)
+    ]
+    for copy in row_copies + left_copies + right_copies:
         copy.start()
 
     def gather_tile(tile, total):
@@ -137,10 +180,11 @@
             block[at, x * share : (x + 1) * share] = both.astype(block.dtype)
         return total
 
-    grad_sum = lax.fori_loop(
-        0, tiles, gather_tile, jnp.zeros((pair, share), jnp.float32)
-    )
-    for copy, unused in copies:
+    grad_sum = jnp.zeros((pair, share), jnp.float32)
+    for y in range(grid_y):
+        row_copies[y].wait()
+        grad_sum = lax.fori_loop(y * grid_z, (y + 1) * grid_z, gather_tile, grad_sum)
+    for copy in left_copies:
         copy.wait()
 
     def mix(tile, carry):
@@ -152,7 +196,7 @@
         return carry
 
     lax.fori_loop(0, grid_x, mix, 0)
-    for unused, copy in copies:
+    for copy in right_copies:
         copy.wait()
 
     def finish(x, total):
@@ -175,33 +219,40 @@
         for x in range(grid_x):
             scaled = (product[x, at, :] * factor).reshape(grid_core, row_local, share)
             for core in range(grid_core):
-                out[(y * grid_core + core) * grid_x + x, z] = scaled[core].astype(out.dtype)
-        return carry
-
-    lax.fori_loop(0, tiles, scatter_tile, 0)
-
-
-def precondition_slot(here, core, rows, left_root, right_root, left_pieces, right_pieces):
+                staged[(y * grid_core + core) * grid_x + x, z] = scaled[core].astype(out.dtype)
+        return carry
+
+    out_copies = []
+    for y, span in enumerate(spans):
+        lax.fori_loop(y * grid_z, (y + 1) * grid_z, scatter_tile, 0)
+        out_copies.append(
+            pltpu.make_async_copy(staged.at[span], out.at[span], sems.at[last_sem + y])
+        )
+        out_copies[-1].start()
+    for copy in out_copies:
+        copy.wait()
+
+
+def precondition_slot(here, core, rows, left_root, right_root, pieces):
     slots, order = right_root.shape[:2]
     share = order // grid_x
-    any_spec = pl.BlockSpec(memory_space=pl.ANY)
-    vmem_spec = pl.BlockSpec(memory_space=pltpu.VMEM)
+    hbm_spec = pl.BlockSpec(memory_space=pltpu.HBM)
     return pl.pallas_call(
         slot_kernel,
         out_shape=jax.ShapeDtypeStruct(rows.shape, rows.dtype),
-        in_specs=[pl.BlockSpec(memory_space=pltpu.SMEM)]
-        + [vmem_spec]
-        + [any_spec] * (2 * grid_x),
-        out_specs=vmem_spec,
+        in_specs=[pl.BlockSpec(memory_space=pltpu.SMEM)] + [hbm_spec] * (3 + len(pieces)),
+        out_specs=hbm_spec,
         scratch_shapes=[
             pltpu.VMEM((grid_x, share, order), jnp.bfloat16),
             pltpu.VMEM((grid_x, order, share), jnp.bfloat16),
+            pltpu.VMEM(rows.shape, rows.dtype),
             pltpu.VMEM((order, order), jnp.bfloat16),
             pltpu.VMEM((order, order), jnp.bfloat16),
             pltpu.VMEM((grid_x, order, share), jnp.float32),
-            pltpu.SemaphoreType.DMA((2 * grid_x,)),
+            pltpu.VMEM(rows.shape, rows.dtype),
+            pltpu.SemaphoreType.DMA((last_sem + 2 * grid_y,)),
         ],
-        compiler_params=pltpu.CompilerParams(vmem_limit_bytes=40 * 1024 * 1024),
+        compiler_params=pltpu.CompilerParams(vmem_limit_bytes=60 * 1024 * 1024),
         cost_estimate=pl.CostEstimate(
             flops=4 * order**3, bytes_accessed=8 * order * order, transcendentals=0
         ),
@@ -210,9 +261,8 @@
         jnp.stack([here, jnp.minimum(slot_at(here, core), slots - 1)]),
         rows,
         left_root,
-        *left_pieces,
         right_root,
-        *right_pieces,
+        *pieces,
     )
 
 
@@ -221,8 +271,7 @@
     slots_each = left_root.shape[0]
     chunk = (row_local, col_local)
     here, core = lax.axis_index("x"), lax.axis_index("core")
-    left_pieces = factor_pieces(left_root, here, core)
-    right_pieces = factor_pieces(right_root, here, core)
+    pieces = factor_pieces(left_root, right_root, here, core)
 
     owner = assignment // slots_each
     plane = (owner // grid_core) % grid_z
@@ -250,15 +299,11 @@
         return lax.all_to_all(rows, plane_axes, 0, 0, tiled=True)
 
     rows = vmem_call(pick_kernel, [block_at], [gradients], z_rows, "pick_for_z")
-    rows, left_pieces, right_pieces = lax.optimization_barrier(
-        (z_hop(rows), left_pieces, right_pieces)
-    )
+    rows, pieces = lax.optimization_barrier((z_hop(rows), pieces))
     kernel = functools.partial(pick_runs_kernel, (1, plane_cap, grid_z, 1))
     rows = vmem_call(kernel, [rank_at], [rows], plane_rows, "pick_for_plane")
     rows = plane_hop(rows)
-    update = precondition_slot(
-        here, core, rows, left_root, right_root, left_pieces, right_pieces
-    )
+    update = precondition_slot(here, core, rows, left_root, right_root, pieces)
     update = plane_hop(update).reshape((plane_rows,) + chunk)
     kernel = functools.partial(pick_runs_kernel, (grid_z, 1, 1, plane_cap))
     update = vmem_call(kernel, [holder_at], [update], z_rows, "pick_back_for_z")

time: 235 us -> 221 us (0.940)
  local copies, waits for them, and re-layouts: 10.8 us -> 1.02 us
  blocking collectives: 71 us -> 62.1 us
  waiting for transfers between devices: 86.1 us -> 94.7 us
  starting transfers between devices: 44.1 us -> 37 us
  Pallas kernels: 15.9 us -> 19.7 us
    ppermute x6 -> x3, waiting for transfers between devices: 34.6 us -> 43.8 us  [factor_pieces(): got.append(lax.ppermute(piece, ('core', 'x'), pairs))]
    all_to_all x1, blocking collectives: 71 us -> 62.1 us  [z_hop(): lax.all_to_all(rows, 'z', 0, 0, tiled=True).reshape((z_rows,) + chunk)]
    ppermute x6 -> x3, starting transfers between devices: 14.9 us -> 7.76 us  [factor_pieces(): got.append(lax.ppermute(piece, ('core', 'x'), pairs))]
    cond x22 -> x12, local copies, waits for them, and re-layouts: 7.87 us -> 1.02 us
    squeeze x2 -> x0, local copies, waits for them, and re-layouts: 2.96 us -> none  [factor_pieces(): piece = lax.dynamic_index_in_dim(factor, slot, 0, keepdims=False)]
  transfers between devices with their start and end apart: 9 -> 6, of which waited for: 6 -> 5; matrix products, arithmetic and copies ran while one was open for 1% -> 0% of each run, Pallas kernels for 0% -> 1%
where the time goes in v2:
time: 221 us; the launch traced here: 220 us
  waiting for transfers between devices  94.7 us (43%)
  blocking collectives  62.1 us (28%)
  starting transfers between devices  37 us (17%)
  Pallas kernels  19.7 us (9%)
  other arithmetic  4.24 us (2%)
    all_to_all x1, blocking collectives, z_hop(): lax.all_to_all(rows, 'z', 0, 0, tiled=True).reshape((z_rows,) + chunk)  62.1 us
    all_to_all x2, waiting for transfers between devices, plane_hop(): return lax.all_to_all(rows, plane_axes, 0, 0, tiled=True)  50.9 us
    ppermute x3, waiting for transfers between devices, factor_pieces(): got.append(lax.ppermute(piece, ('core', 'x'), pairs))  43.8 us
    all_to_all x1, starting transfers between devices, z_hop(): lax.all_to_all(rows, 'z', 0, 0, tiled=True).reshape((z_rows,) + chunk)  15.2 us
    all_to_all x2, starting transfers between devices, plane_hop(): return lax.all_to_all(rows, plane_axes, 0, 0, tiled=True)  14 us
    pallas_call x1, Pallas kernels, precondition_slot(): pl.pallas_call(slot_kernel, out_shape=jax.ShapeDtypeStruct(rows.shape, ro...  10.5 us
    ppermute x3, starting transfers between devices, factor_pieces(): got.append(lax.ppermute(piece, ('core', 'x'), pairs))  7.76 us
    pallas_call x5, Pallas kernels, vmem_call(): pl.pallas_call(kernel, out_shape=jax.ShapeDtypeStruct((count,) + arrays[0...  7.03 us
  transfers between devices with their start and end apart: 6, of which 5 were waited for; matrix products, arithmetic and copies ran while one was open for 0% of the time, Pallas kernels for 1%

profile of v2, /device:TPU:6, one launch (start us, length us, event | category | flops | bytes accessed | tf_op | source)
XLA Modules:
  0.0 220.3 jit_solution(11596867864452333720)
XLA Ops:
  0.6 0.7 and_select_fusion.35
  1.4 0.7 convert_reduce_fusion.6
  3.5 216.8 %conditional.1 = (bf16[128,8,256]{2,1,0:T(8,128)(2,1)}, bf16[128,8,256]{2,1,0:T(8,128)(2,1)}) conditional(s32[]{:T(128)} %clamp.3, (s32[128]{0:T(128)}, bf16[128,8,256]{2,1,0:T(8,128)(2,1)}, bf16[3,256,1024]{2,1,0:T(8,128)(2,1)}, bf16[3,1024,256]{2,1,0:T(8,128)(2,1)}, bf16[128,8,256]{2,1,0:T(8,128)(2,1)}) %tuple.32, ...), branch_computations={%region_3.8_spmd, %region_8.13_spmd, %region_13.18_spmd, %region_1... | conditional | flops 4295227392 | bytes 66595112 | solution.py:324
  3.5 0.8 compare_select_fusion.10
  4.6 2.4 %pick_for_z.6 = bf16[240,8,256]{2,1,0:T(8,128)(2,1)} custom-call(s32[240]{0:T(256)S(1)} %select_reduce_fusion.3.index_ref, bf16[128,8,256]{2,1,0:T(8,128)(2,1)} %get-tuple-element.63.src_ref), custom_call_target="tpu_custom_call" | custom-call | tf_op jit(solution)/shard_map/cond/branch_1_fun/pick_for_z/pallas_call | solution.py:59
  7.1 15.2 %all-to-all-start.4 = ((bf16[16,15,8,256]{3,2,1,0:T(8,128)(2,1)}), bf16[16,15,8,256]{3,2,1,0:T(8,128)(2,1)S(1)}, u32[]{:S(2)}, u32[]{:S(2)}) async-start(bf16[16,15,8,256]{3,2,1,0:T(8,128)(2,1)} %bitcast.13), calls=%async_computation.4 | async-start | bytes 1966080 | tf_op jit(solution)/shard_map/cond/branch_1_fun/all_to_all | solution.py:295
  22.4 2.2 pack_factors.6
  24.6 2.4 %collective-permute-start.3 = (bf16[512,1024]{1,0:T(8,128)(2,1)S(1)}, bf16[512,1024]{1,0:T(8,128)(2,1)S(1)}, u32[]{:S(2)}, u32[]{:S(2)}) collective-permute-start(bf16[512,1024]{1,0:T(8,128)(2,1)S(1)} %get-tuple-element.66), channel_id=1, source_target_pairs={{1,2},{2,3},{3,0},{4,5},{6,7},{7,4},{9,10},{10,11},{11,8},{12,13},... | collective-permute-start | bytes 3145736 | tf_op jit(solution)/shard_map/cond/branch_1_fun/ppermute | solution.py:127
  26.9 1.3 collective-permute-start.4
  28.2 4.1 %collective-permute-start.5 = (bf16[512,1024]{1,0:T(8,128)(2,1)S(1)}, bf16[512,1024]{1,0:T(8,128)(2,1)}, u32[]{:S(2)}, u32[]{:S(2)}) collective-permute-start(bf16[512,1024]{1,0:T(8,128)(2,1)S(1)} %get-tuple-element.68), channel_id=1, source_target_pairs={{0,3},{1,0},{3,2},{4,7},{5,4},{6,5},{8,11},{9,8},{11,10},{12,15},{... | collective-permute-start | bytes 3145736 | tf_op jit(solution)/shard_map/cond/branch_1_fun/ppermute | solution.py:127
  32.5 20.1 %collective-permute-done.3.refs_3_ = bf16[512,1024]{1,0:T(8,128)(2,1)S(1)} collective-permute-done((bf16[512,1024]{1,0:T(8,128)(2,1)S(1)}, bf16[512,1024]{1,0:T(8,128)(2,1)S(1)}, u32[]{:S(2)}, u32[]{:S(2)}) %collective-permute-start.3) | collective-permute-done | bytes 1048608 | tf_op jit(solution)/shard_map/cond/branch_1_fun/ppermute | solution.py:127
  52.5 4.0 %collective-permute-done.4.refs_4_ = bf16[512,1024]{1,0:T(8,128)(2,1)S(1)} collective-permute-done((bf16[512,1024]{1,0:T(8,128)(2,1)S(1)}, bf16[512,1024]{1,0:T(8,128)(2,1)S(1)}, u32[]{:S(2)}, u32[]{:S(2)}) %collective-permute-start.4) | collective-permute-done | bytes 1048608 | tf_op jit(solution)/shard_map/cond/branch_1_fun/ppermute | solution.py:127
  56.5 1.0 copy-done.26
  57.5 19.8 %collective-permute-done.5.refs_5_ = bf16[512,1024]{1,0:T(8,128)(2,1)} collective-permute-done((bf16[512,1024]{1,0:T(8,128)(2,1)S(1)}, bf16[512,1024]{1,0:T(8,128)(2,1)}, u32[]{:S(2)}, u32[]{:S(2)}) %collective-permute-start.5) | collective-permute-done | bytes 1048608 | tf_op jit(solution)/shard_map/cond/branch_1_fun/ppermute | solution.py:127
  77.3 2.1 pick_for_plane.6
  79.4 7.5 %all-to-all-start.5 = ((bf16[32,16,8,256]{3,2,1,0:T(8,128)(2,1)}), bf16[32,16,8,256]{3,2,1,0:T(8,128)(2,1)}, u32[]{:S(2)}, u32[]{:S(2)}) async-start(bf16[32,16,8,256]{3,2,1,0:T(8,128)(2,1)} %bitcast.18), calls=%async_computation.5 | async-start | bytes 4194304 | tf_op jit(solution)/shard_map/cond/branch_1_fun/all_to_all | solution.py:299
  87.6 25.2 %all-to-all-done.5.refs_0_ = bf16[32,16,8,256]{3,2,1,0:T(8,128)(2,1)} async-done(((bf16[32,16,8,256]{3,2,1,0:T(8,128)(2,1)}), bf16[32,16,8,256]{3,2,1,0:T(8,128)(2,1)}, u32[]{:S(2)}, u32[]{:S(2)}) %all-to-all-start.5) | async-done | bytes 2097184 | tf_op jit(solution)/shard_map/cond/branch_1_fun/all_to_all | solution.py:299
  112.8 10.5 %precondition_slot.6 = bf16[32,16,8,256]{3,2,1,0:T(8,128)(2,1)} custom-call(s32[2]{0:T(128)} %pad_add_fusion.2.here_ref, bf16[32,16,8,256]{3,2,1,0:T(8,128)(2,1)} %all-to-all-done.5.refs_0_, bf16[3,256,1024]{2,1,0:T(8,128)(2,1)S(1)} %copy-done.1, bf16[3,1024,256]{2,1,0:T(8,128)(2,1)S(1)} %copy-done.6, bf16[512,1024]{1,0:T(8,128)(2,1)} %copy-done.21, ...), custom_call_target="tpu_custom_call" | custom-call | flops 4294967296 | bytes 8388608 | tf_op jit(solution)/shard_map/cond/branch_1_fun/precondition_slot/pallas_call | solution.py:240
  123.3 6.5 %all-to-all-start.6 = ((bf16[32,16,8,256]{3,2,1,0:T(8,128)(2,1)}), bf16[32,16,8,256]{3,2,1,0:T(8,128)(2,1)S(1)}, u32[]{:S(2)}, u32[]{:S(2)}) async-start(bf16[32,16,8,256]{3,2,1,0:T(8,128)(2,1)} %precondition_slot.6), calls=%async_computation.6 | async-start | bytes 4194304 | tf_op jit(solution)/shard_map/cond/branch_1_fun/all_to_all | solution.py:299
  130.0 25.7 %all-to-all-done.6 = bf16[32,16,8,256]{3,2,1,0:T(8,128)(2,1)S(1)} async-done(((bf16[32,16,8,256]{3,2,1,0:T(8,128)(2,1)}), bf16[32,16,8,256]{3,2,1,0:T(8,128)(2,1)S(1)}, u32[]{:S(2)}, u32[]{:S(2)}) %all-to-all-start.6) | async-done | bytes 2097184 | tf_op jit(solution)/shard_map/cond/branch_1_fun/all_to_all | solution.py:299
  155.7 0.7 pick_back_for_z.6
  156.4 62.1 %all_to_all.81 = bf16[16,15,8,256]{3,2,1,0:T(8,128)(2,1)S(1)} all-to-all(bf16[16,15,8,256]{3,2,1,0:T(8,128)(2,1)S(1)} %bitcast.70), channel_id=1, replica_groups=mesh['y'=4,'z'=16,'core'=2,'x'=4] {'z'}, dimensions={0} | all-to-all | bytes 1966080 | tf_op jit(solution)/shard_map/cond/branch_1_fun/all_to_all | solution.py:295
  218.5 0.8 pick_step_rows.6.step_ref
  219.3 1.0 step.6
  (21 shorter events, 2.0 us)
Async XLA Ops:
  3.5 18.9 %copy-start.1 = (bf16[3,256,1024]{2,1,0:T(8,128)(2,1)S(1)}, bf16[3,256,1024]{2,1,0:T(8,128)(2,1)}, u32[]{:S(2)}) copy-start(bf16[3,256,1024]{2,1,0:T(8,128)(2,1)} %get-tuple-element.64.left_ref.refs_1_) | copy-start | bytes 4718596 | tf_op jit(solution)/shard_map/cond
  7.1 70.2 %all-to-all-start.4 = ((bf16[16,15,8,256]{3,2,1,0:T(8,128)(2,1)}), bf16[16,15,8,256]{3,2,1,0:T(8,128)(2,1)S(1)}, u32[]{:S(2)}, u32[]{:S(2)}) async-start(bf16[16,15,8,256]{3,2,1,0:T(8,128)(2,1)} %bitcast.13), calls=%async_computation.4 | async-start | bytes 1966080 | tf_op jit(solution)/shard_map/cond/branch_1_fun/all_to_all | solution.py:295
  24.6 28.0 %collective-permute-start.3 = (bf16[512,1024]{1,0:T(8,128)(2,1)S(1)}, bf16[512,1024]{1,0:T(8,128)(2,1)S(1)}, u32[]{:S(2)}, u32[]{:S(2)}) collective-permute-start(bf16[512,1024]{1,0:T(8,128)(2,1)S(1)} %get-tuple-element.66), channel_id=1, source_target_pairs={{1,2},{2,3},{3,0},{4,5},{6,7},{7,4},{9,10},{10,11},{11,8},{12,13},... | collective-permute-start | bytes 3145736 | tf_op jit(solution)/shard_map/cond/branch_1_fun/ppermute | solution.py:127
  26.9 29.5 %collective-permute-start.4 = (bf16[512,1024]{1,0:T(8,128)(2,1)S(1)}, bf16[512,1024]{1,0:T(8,128)(2,1)S(1)}, u32[]{:S(2)}, u32[]{:S(2)}) collective-permute-start(bf16[512,1024]{1,0:T(8,128)(2,1)S(1)} %get-tuple-element.67), channel_id=1, source_target_pairs={{0,2},{1,3},{2,0},{5,7},{6,4},{7,5},{8,10},{9,11},{10,8},{13,15},{... | collective-permute-start | bytes 3145736 | tf_op jit(solution)/shard_map/cond/branch_1_fun/ppermute | solution.py:127
  28.2 49.0 %collective-permute-start.5 = (bf16[512,1024]{1,0:T(8,128)(2,1)S(1)}, bf16[512,1024]{1,0:T(8,128)(2,1)}, u32[]{:S(2)}, u32[]{:S(2)}) collective-permute-start(bf16[512,1024]{1,0:T(8,128)(2,1)S(1)} %get-tuple-element.68), channel_id=1, source_target_pairs={{0,3},{1,0},{3,2},{4,7},{5,4},{6,5},{8,11},{9,8},{11,10},{12,15},{... | collective-permute-start | bytes 3145736 | tf_op jit(solution)/shard_map/cond/branch_1_fun/ppermute | solution.py:127
  52.5 4.0 %copy-start.21 = (bf16[512,1024]{1,0:T(8,128)(2,1)}, bf16[512,1024]{1,0:T(8,128)(2,1)S(1)}, u32[]{:S(2)}) copy-start(bf16[512,1024]{1,0:T(8,128)(2,1)S(1)} %collective-permute-done.3.refs_3_) | copy-start | bytes 3145732 | tf_op jit(solution)/shard_map/cond
  56.5 1.0 copy-start.26
  79.4 33.4 %copy-start.6 = (bf16[3,1024,256]{2,1,0:T(8,128)(2,1)S(1)}, bf16[3,1024,256]{2,1,0:T(8,128)(2,1)}, u32[]{:S(2)}) copy-start(bf16[3,1024,256]{2,1,0:T(8,128)(2,1)} %get-tuple-element.65.right_ref.refs_2_) | copy-start | bytes 4718596 | tf_op jit(solution)/shard_map/cond
  79.4 33.4 %all-to-all-start.5 = ((bf16[32,16,8,256]{3,2,1,0:T(8,128)(2,1)}), bf16[32,16,8,256]{3,2,1,0:T(8,128)(2,1)}, u32[]{:S(2)}, u32[]{:S(2)}) async-start(bf16[32,16,8,256]{3,2,1,0:T(8,128)(2,1)} %bitcast.18), calls=%async_computation.5 | async-start | bytes 4194304 | tf_op jit(solution)/shard_map/cond/branch_1_fun/all_to_all | solution.py:299
  123.3 32.4 %all-to-all-start.6 = ((bf16[32,16,8,256]{3,2,1,0:T(8,128)(2,1)}), bf16[32,16,8,256]{3,2,1,0:T(8,128)(2,1)S(1)}, u32[]{:S(2)}, u32[]{:S(2)}) async-start(bf16[32,16,8,256]{3,2,1,0:T(8,128)(2,1)} %precondition_slot.6), calls=%async_computation.6 | async-start | bytes 4194304 | tf_op jit(solution)/shard_map/cond/branch_1_fun/all_to_all | solution.py:299
  156.4 62.9 %copy-start.16 = (bf16[128,8,256]{2,1,0:T(8,128)(2,1)S(1)}, bf16[128,8,256]{2,1,0:T(8,128)(2,1)}, u32[]{:S(2)}) copy-start(bf16[128,8,256]{2,1,0:T(8,128)(2,1)} %get-tuple-element.73.parameter_ref) | copy-start | bytes 1572868 | tf_op jit(solution)/shard_map/cond
  219.2 1.1 copy-start.11

commit v3 on v2

--- a/solution.py
+++ b/solution.py
@@ -13,7 +13,7 @@
 plane_axes = ("y", "core", "x")
 fsdp_axes = ("y", "z", "core")
 plane_devices = grid_y * grid_core * grid_x
-plane_capacities = (13, 15, 16, 18, 24)
+plane_capacities = (13, 14, 15, 16, 18, 24)
 
 pick_run = 8
 
@@ -69,6 +69,9 @@
 def place(values, keys, size):
     hit = jnp.arange(size, dtype=jnp.int32)[:, None] == keys[None, :]
     return jnp.sum(jnp.where(hit, values[None, :], 0), axis=1)
+
+
+piece_shifts = (2, 3, 1)
 
 
 def holder_x(slot, core):
@@ -104,20 +107,21 @@
 
 def factor_pieces(left_root, right_root, here, core):
     slots, share, order = left_root.shape
-    shifts = range(1, grid_x)
-    wanted = jnp.stack([jnp.minimum(slot_at(here + shift, core), slots - 1) for shift in shifts])
+    wanted = jnp.stack(
+        [jnp.minimum(slot_at(here + shift, core), slots - 1) for shift in piece_shifts]
+    )
     hbm_spec = pl.BlockSpec(memory_space=pltpu.HBM)
     packed = pl.pallas_call(
         pack_kernel,
-        out_shape=[jax.ShapeDtypeStruct((2 * share, order), left_root.dtype) for shift in shifts],
+        out_shape=[jax.ShapeDtypeStruct((2 * share, order), left_root.dtype)] * len(piece_shifts),
         in_specs=[pl.BlockSpec(memory_space=pltpu.SMEM), hbm_spec, hbm_spec],
-        out_specs=[pl.BlockSpec(memory_space=pltpu.VMEM)] * len(shifts),
-        scratch_shapes=[pltpu.SemaphoreType.DMA((len(shifts) * (grid_x + 1),))],
+        out_specs=[pl.BlockSpec(memory_space=pltpu.VMEM)] * len(piece_shifts),
+        scratch_shapes=[pltpu.SemaphoreType.DMA((len(piece_shifts) * (grid_x + 1),))],
         compiler_params=pltpu.CompilerParams(vmem_limit_bytes=32 * 1024 * 1024),
         name="pack_factors",
     )(wanted, left_root, right_root)
     got = []
-    for shift, piece in zip(shifts, packed):
+    for shift, piece in zip(piece_shifts, packed):
         pairs = [
             (at * grid_x + src, at * grid_x + (src + shift) % grid_x)
             for at in range(grid_core)
@@ -143,10 +147,9 @@
     tiles = order // pair
     left_copies = [pltpu.make_async_copy(own_left.at[slot], left.at[here], sems.at[0])]
     right_copies = [pltpu.make_async_copy(own_right.at[slot], right.at[here], sems.at[1])]
-    for piece in pieces:
-        shift = len(left_copies)
-        at = lax.rem(here - shift + grid_x, grid_x)
-        first = 2 + (shift - 1) * (grid_x + 1)
+    for number, piece in enumerate(pieces):
+        at = lax.rem(here - piece_shifts[number] + grid_x, grid_x)
+        first = 2 + number * (grid_x + 1)
         left_copies.append(
             pltpu.make_async_copy(piece.at[:share], left.at[at], sems.at[first])
         )
@@ -189,10 +192,9 @@
 
     def mix(tile, carry):
         at = pl.ds(pl.multiple_of(tile * share, share), share)
-        for x in range(grid_x):
-            mixed[x * share : (x + 1) * share, at] = jnp.dot(
-                left[x], block[:, at], preferred_element_type=jnp.float32
-            ).astype(mixed.dtype)
+        mixed[:, at] = jnp.dot(
+            left[...].reshape(order, order), block[:, at], preferred_element_type=jnp.float32
+        ).astype(mixed.dtype)
         return carry
 
     lax.fori_loop(0, grid_x, mix, 0)
@@ -200,12 +202,9 @@
         copy.wait()
 
     def finish(x, total):
-        for tile in range(grid_x):
-            at = slice(tile * share, (tile + 1) * share)
-            part = jnp.dot(mixed[at, :], right[x], preferred_element_type=jnp.float32)
-            product[x, at] = part
-            total = total + jnp.sum(jnp.square(part), axis=0, keepdims=True)
-        return total
+        part = jnp.dot(mixed[...], right[x], preferred_element_type=jnp.float32)
+        product[x] = part
+        return total + jnp.sum(jnp.square(part), axis=0, keepdims=True)
 
     update_sum = lax.fori_loop(0, grid_x, finish, jnp.zeros((1, share), jnp.float32))
     entries = float(order * order)
@@ -318,8 +317,7 @@
     loads = jnp.sum(
         (plane[None, :] == jnp.arange(grid_z, dtype=jnp.int32)[:, None]).astype(jnp.int32), axis=1
     )
-    caps = jnp.array(plane_capacities[:-1], jnp.int32)
-    choice = jnp.max(jnp.sum((loads[:, None] > caps[None, :]).astype(jnp.int32), axis=1))
+    choice = jnp.max(sum((loads > cap).astype(jnp.int32) for cap in plane_capacities[:-1]))
     branches = [functools.partial(program, cap) for cap in plane_capacities]
     return lax.switch(choice, branches, gradients, parameters, left_root, right_root, assignment)
 

time: 221 us -> 219 us (level)
  waiting for transfers between devices: 94.7 us -> 92.1 us
    ppermute x3, waiting for transfers between devices: 43.8 us -> 41.1 us  [factor_pieces(): got.append(lax.ppermute(piece, ('core', 'x'), pairs))]
  transfers between devices with their start and end apart: 6 -> 6, of which waited for: 5 -> 4; matrix products, arithmetic and copies ran while one was open for 0% -> 0% of each run, Pallas kernels for 1% -> 1%
where the time goes in v3:
time: 219 us; the launch traced here: 218 us
  waiting for transfers between devices  92.1 us (42%)
  blocking collectives  62.1 us (28%)
  starting transfers between devices  38.5 us (18%)
  Pallas kernels  19.7 us (9%)
  other arithmetic  3.44 us (2%)
    all_to_all x1, blocking collectives, z_hop(): lax.all_to_all(rows, 'z', 0, 0, tiled=True).reshape((z_rows,) + chunk)  62.1 us
    all_to_all x2, waiting for transfers between devices, plane_hop(): return lax.all_to_all(rows, plane_axes, 0, 0, tiled=True)  51 us
    ppermute x3, waiting for transfers between devices, factor_pieces(): got.append(lax.ppermute(piece, ('core', 'x'), pairs))  41.1 us
    all_to_all x1, starting transfers between devices, z_hop(): lax.all_to_all(rows, 'z', 0, 0, tiled=True).reshape((z_rows,) + chunk)  15.2 us
    all_to_all x2, starting transfers between devices, plane_hop(): return lax.all_to_all(rows, plane_axes, 0, 0, tiled=True)  14 us
    pallas_call x1, Pallas kernels, precondition_slot(): pl.pallas_call(slot_kernel, out_shape=jax.ShapeDtypeStruct(rows.shape, ro...  10.5 us
    ppermute x3, starting transfers between devices, factor_pieces(): got.append(lax.ppermute(piece, ('core', 'x'), pairs))  9.24 us
    pallas_call x5, Pallas kernels, vmem_call(): pl.pallas_call(kernel, out_shape=jax.ShapeDtypeStruct((count,) + arrays[0...  7.06 us
  transfers between devices with their start and end apart: 6, of which 4 were waited for; matrix products, arithmetic and copies ran while one was open for 0% of the time, Pallas kernels for 1%

profile of v3, /device:TPU:6, one launch (start us, length us, event | category | flops | bytes accessed | tf_op | source)
XLA Modules:
  0.0 218.3 jit_solution(5937886652441172637)
XLA Ops:
  0.6 0.7 and_select_fusion.42
  1.4 0.6 fusion.40
  2.7 215.6 %conditional.1 = (bf16[128,8,256]{2,1,0:T(8,128)(2,1)}, bf16[128,8,256]{2,1,0:T(8,128)(2,1)}) conditional(s32[]{:T(128)} %clamp.3, (s32[128]{0:T(128)}, bf16[128,8,256]{2,1,0:T(8,128)(2,1)}, bf16[3,256,1024]{2,1,0:T(8,128)(2,1)}, bf16[3,1024,256]{2,1,0:T(8,128)(2,1)}, bf16[128,8,256]{2,1,0:T(8,128)(2,1)}) %tuple.37, ...), branch_computations={%region_2.7_spmd, %region_7.12_spmd, %region_12.17_spmd, %region_1... | conditional | flops 4295227392 | bytes 66595112 | solution.py:322
  2.8 0.8 compare_select_fusion.16
  3.9 2.5 %pick_for_z.8 = bf16[240,8,256]{2,1,0:T(8,128)(2,1)} custom-call(s32[240]{0:T(256)S(1)} %select_reduce_fusion.6.index_ref, bf16[128,8,256]{2,1,0:T(8,128)(2,1)} %get-tuple-element.85.src_ref), custom_call_target="tpu_custom_call" | custom-call | tf_op jit(solution)/shard_map/cond/branch_2_fun/pick_for_z/pallas_call | solution.py:59
  6.3 15.2 %all-to-all-start.8 = ((bf16[16,15,8,256]{3,2,1,0:T(8,128)(2,1)}), bf16[16,15,8,256]{3,2,1,0:T(8,128)(2,1)S(1)}, u32[]{:S(2)}, u32[]{:S(2)}) async-start(bf16[16,15,8,256]{3,2,1,0:T(8,128)(2,1)} %bitcast.24), calls=%async_computation.8 | async-start | bytes 1966080 | tf_op jit(solution)/shard_map/cond/branch_2_fun/all_to_all | solution.py:294
  21.7 2.2 pack_factors.8
  23.8 1.3 collective-permute-start.6
  25.1 3.9 %collective-permute-start.7 = (bf16[512,1024]{1,0:T(8,128)(2,1)S(1)}, bf16[512,1024]{1,0:T(8,128)(2,1)S(1)}, u32[]{:S(2)}, u32[]{:S(2)}) collective-permute-start(bf16[512,1024]{1,0:T(8,128)(2,1)S(1)} %get-tuple-element.89), channel_id=1, source_target_pairs={{0,3},{1,0},{3,2},{4,7},{5,4},{6,5},{8,11},{9,8},{11,10},{12,15},{... | collective-permute-start | bytes 3145736 | tf_op jit(solution)/shard_map/cond/branch_2_fun/ppermute | solution.py:131
  29.0 4.1 %collective-permute-start.8 = (bf16[512,1024]{1,0:T(8,128)(2,1)S(1)}, bf16[512,1024]{1,0:T(8,128)(2,1)}, u32[]{:S(2)}, u32[]{:S(2)}) collective-permute-start(bf16[512,1024]{1,0:T(8,128)(2,1)S(1)} %get-tuple-element.90), channel_id=1, source_target_pairs={{1,2},{2,3},{3,0},{4,5},{6,7},{7,4},{9,10},{10,11},{11,8},{12,13},... | collective-permute-start | bytes 3145736 | tf_op jit(solution)/shard_map/cond/branch_2_fun/ppermute | solution.py:131
  33.2 20.1 %collective-permute-done.6.refs_3_ = bf16[512,1024]{1,0:T(8,128)(2,1)S(1)} collective-permute-done((bf16[512,1024]{1,0:T(8,128)(2,1)S(1)}, bf16[512,1024]{1,0:T(8,128)(2,1)S(1)}, u32[]{:S(2)}, u32[]{:S(2)}) %collective-permute-start.6) | collective-permute-done | bytes 1048608 | tf_op jit(solution)/shard_map/cond/branch_2_fun/ppermute | solution.py:131
  53.4 21.0 %collective-permute-done.7.refs_4_ = bf16[512,1024]{1,0:T(8,128)(2,1)S(1)} collective-permute-done((bf16[512,1024]{1,0:T(8,128)(2,1)S(1)}, bf16[512,1024]{1,0:T(8,128)(2,1)S(1)}, u32[]{:S(2)}, u32[]{:S(2)}) %collective-permute-start.7) | collective-permute-done | bytes 1048608 | tf_op jit(solution)/shard_map/cond/branch_2_fun/ppermute | solution.py:131
  74.3 1.0 copy-done.32
  75.3 2.1 pick_for_plane.8
  77.5 7.5 %all-to-all-start.9 = ((bf16[32,16,8,256]{3,2,1,0:T(8,128)(2,1)}), bf16[32,16,8,256]{3,2,1,0:T(8,128)(2,1)}, u32[]{:S(2)}, u32[]{:S(2)}) async-start(bf16[32,16,8,256]{3,2,1,0:T(8,128)(2,1)} %bitcast.29), calls=%async_computation.9 | async-start | bytes 4194304 | tf_op jit(solution)/shard_map/cond/branch_2_fun/all_to_all | solution.py:298
  85.0 0.6 pad_add_fusion.4.here_ref
  85.6 25.3 %all-to-all-done.9.refs_0_ = bf16[32,16,8,256]{3,2,1,0:T(8,128)(2,1)} async-done(((bf16[32,16,8,256]{3,2,1,0:T(8,128)(2,1)}), bf16[32,16,8,256]{3,2,1,0:T(8,128)(2,1)}, u32[]{:S(2)}, u32[]{:S(2)}) %all-to-all-start.9) | async-done | bytes 2097184 | tf_op jit(solution)/shard_map/cond/branch_2_fun/all_to_all | solution.py:298
  110.9 10.5 %precondition_slot.8 = bf16[32,16,8,256]{3,2,1,0:T(8,128)(2,1)} custom-call(s32[2]{0:T(128)} %pad_add_fusion.4.here_ref, bf16[32,16,8,256]{3,2,1,0:T(8,128)(2,1)} %all-to-all-done.9.refs_0_, bf16[3,256,1024]{2,1,0:T(8,128)(2,1)S(1)} %copy-done.2, bf16[3,1024,256]{2,1,0:T(8,128)(2,1)S(1)} %copy-done.8, bf16[512,1024]{1,0:T(8,128)(2,1)} %copy-done.26, ...), custom_call_target="tpu_custom_call" | custom-call | flops 4294967296 | bytes 8388608 | tf_op jit(solution)/shard_map/cond/branch_2_fun/precondition_slot/pallas_call | solution.py:239
  121.4 6.5 %all-to-all-start.10 = ((bf16[32,16,8,256]{3,2,1,0:T(8,128)(2,1)}), bf16[32,16,8,256]{3,2,1,0:T(8,128)(2,1)S(1)}, u32[]{:S(2)}, u32[]{:S(2)}) async-start(bf16[32,16,8,256]{3,2,1,0:T(8,128)(2,1)} %precondition_slot.8), calls=%async_computation.10 | async-start | bytes 4194304 | tf_op jit(solution)/shard_map/cond/branch_2_fun/all_to_all | solution.py:298
  128.0 25.7 %all-to-all-done.10 = bf16[32,16,8,256]{3,2,1,0:T(8,128)(2,1)S(1)} async-done(((bf16[32,16,8,256]{3,2,1,0:T(8,128)(2,1)}), bf16[32,16,8,256]{3,2,1,0:T(8,128)(2,1)S(1)}, u32[]{:S(2)}, u32[]{:S(2)}) %all-to-all-start.10) | async-done | bytes 2097184 | tf_op jit(solution)/shard_map/cond/branch_2_fun/all_to_all | solution.py:298
  153.8 0.7 pick_back_for_z.8
  154.4 62.1 %all_to_all.98 = bf16[16,15,8,256]{3,2,1,0:T(8,128)(2,1)S(1)} all-to-all(bf16[16,15,8,256]{3,2,1,0:T(8,128)(2,1)S(1)} %bitcast.82), channel_id=1, replica_groups=mesh['y'=4,'z'=16,'core'=2,'x'=4] {'z'}, dimensions={0} | all-to-all | bytes 1966080 | tf_op jit(solution)/shard_map/cond/branch_2_fun/all_to_all | solution.py:294
  216.5 0.8 pick_step_rows.8.step_ref
  217.3 1.0 step.8
  (20 shorter events, 0.7 us)
Async XLA Ops:
  2.8 18.9 %copy-start.2 = (bf16[3,256,1024]{2,1,0:T(8,128)(2,1)S(1)}, bf16[3,256,1024]{2,1,0:T(8,128)(2,1)}, u32[]{:S(2)}) copy-start(bf16[3,256,1024]{2,1,0:T(8,128)(2,1)} %get-tuple-element.86.left_ref.refs_1_) | copy-start | bytes 4718596 | tf_op jit(solution)/shard_map/cond
  6.3 69.0 %all-to-all-start.8 = ((bf16[16,15,8,256]{3,2,1,0:T(8,128)(2,1)}), bf16[16,15,8,256]{3,2,1,0:T(8,128)(2,1)S(1)}, u32[]{:S(2)}, u32[]{:S(2)}) async-start(bf16[16,15,8,256]{3,2,1,0:T(8,128)(2,1)} %bitcast.24), calls=%async_computation.8 | async-start | bytes 1966080 | tf_op jit(solution)/shard_map/cond/branch_2_fun/all_to_all | solution.py:294
  23.8 29.5 %collective-permute-start.6 = (bf16[512,1024]{1,0:T(8,128)(2,1)S(1)}, bf16[512,1024]{1,0:T(8,128)(2,1)S(1)}, u32[]{:S(2)}, u32[]{:S(2)}) collective-permute-start(bf16[512,1024]{1,0:T(8,128)(2,1)S(1)} %get-tuple-element.88), channel_id=1, source_target_pairs={{0,2},{1,3},{2,0},{5,7},{6,4},{7,5},{8,10},{9,11},{10,8},{13,15},{... | collective-permute-start | bytes 3145736 | tf_op jit(solution)/shard_map/cond/branch_2_fun/ppermute | solution.py:131
  25.1 49.2 %collective-permute-start.7 = (bf16[512,1024]{1,0:T(8,128)(2,1)S(1)}, bf16[512,1024]{1,0:T(8,128)(2,1)S(1)}, u32[]{:S(2)}, u32[]{:S(2)}) collective-permute-start(bf16[512,1024]{1,0:T(8,128)(2,1)S(1)} %get-tuple-element.89), channel_id=1, source_target_pairs={{0,3},{1,0},{3,2},{4,7},{5,4},{6,5},{8,11},{9,8},{11,10},{12,15},{... | collective-permute-start | bytes 3145736 | tf_op jit(solution)/shard_map/cond/branch_2_fun/ppermute | solution.py:131
  29.0 46.3 %collective-permute-start.8 = (bf16[512,1024]{1,0:T(8,128)(2,1)S(1)}, bf16[512,1024]{1,0:T(8,128)(2,1)}, u32[]{:S(2)}, u32[]{:S(2)}) collective-permute-start(bf16[512,1024]{1,0:T(8,128)(2,1)S(1)} %get-tuple-element.90), channel_id=1, source_target_pairs={{1,2},{2,3},{3,0},{4,5},{6,7},{7,4},{9,10},{10,11},{11,8},{12,13},... | collective-permute-start | bytes 3145736 | tf_op jit(solution)/shard_map/cond/branch_2_fun/ppermute | solution.py:131
  53.4 21.0 %copy-start.26 = (bf16[512,1024]{1,0:T(8,128)(2,1)}, bf16[512,1024]{1,0:T(8,128)(2,1)S(1)}, u32[]{:S(2)}) copy-start(bf16[512,1024]{1,0:T(8,128)(2,1)S(1)} %collective-permute-done.6.refs_3_) | copy-start | bytes 3145732 | tf_op jit(solution)/shard_map/cond
  74.3 1.0 copy-start.32
  77.5 33.4 %copy-start.8 = (bf16[3,1024,256]{2,1,0:T(8,128)(2,1)S(1)}, bf16[3,1024,256]{2,1,0:T(8,128)(2,1)}, u32[]{:S(2)}) copy-start(bf16[3,1024,256]{2,1,0:T(8,128)(2,1)} %get-tuple-element.87.right_ref.refs_2_) | copy-start | bytes 4718596 | tf_op jit(solution)/shard_map/cond
  77.5 33.4 %all-to-all-start.9 = ((bf16[32,16,8,256]{3,2,1,0:T(8,128)(2,1)}), bf16[32,16,8,256]{3,2,1,0:T(8,128)(2,1)}, u32[]{:S(2)}, u32[]{:S(2)}) async-start(bf16[32,16,8,256]{3,2,1,0:T(8,128)(2,1)} %bitcast.29), calls=%async_computation.9 | async-start | bytes 4194304 | tf_op jit(solution)/shard_map/cond/branch_2_fun/all_to_all | solution.py:298
  121.4 32.4 %all-to-all-start.10 = ((bf16[32,16,8,256]{3,2,1,0:T(8,128)(2,1)}), bf16[32,16,8,256]{3,2,1,0:T(8,128)(2,1)S(1)}, u32[]{:S(2)}, u32[]{:S(2)}) async-start(bf16[32,16,8,256]{3,2,1,0:T(8,128)(2,1)} %precondition_slot.8), calls=%async_computation.10 | async-start | bytes 4194304 | tf_op jit(solution)/shard_map/cond/branch_2_fun/all_to_all | solution.py:298
  154.4 62.9 %copy-start.20 = (bf16[128,8,256]{2,1,0:T(8,128)(2,1)S(1)}, bf16[128,8,256]{2,1,0:T(8,128)(2,1)}, u32[]{:S(2)}) copy-start(bf16[128,8,256]{2,1,0:T(8,128)(2,1)} %get-tuple-element.95.parameter_ref) | copy-start | bytes 1572868 | tf_op jit(solution)/shard_map/cond
  217.3 1.1 copy-start.14

commit v4 on v3

--- a/solution.py
+++ b/solution.py
@@ -186,7 +186,9 @@
     grad_sum = jnp.zeros((pair, share), jnp.float32)
     for y in range(grid_y):
         row_copies[y].wait()
-        grad_sum = lax.fori_loop(y * grid_z, (y + 1) * grid_z, gather_tile, grad_sum)
+        grad_sum = lax.fori_loop(
+            y * grid_z, (y + 1) * grid_z, gather_tile, grad_sum, unroll=4
+        )
     for copy in left_copies:
         copy.wait()
 
@@ -223,7 +225,7 @@
 
     out_copies = []
     for y, span in enumerate(spans):
-        lax.fori_loop(y * grid_z, (y + 1) * grid_z, scatter_tile, 0)
+        lax.fori_loop(y * grid_z, (y + 1) * grid_z, scatter_tile, 0, unroll=4)
         out_copies.append(
             pltpu.make_async_copy(staged.at[span], out.at[span], sems.at[last_sem + y])
         )
@@ -298,9 +300,9 @@
         return lax.all_to_all(rows, plane_axes, 0, 0, tiled=True)
 
     rows = vmem_call(pick_kernel, [block_at], [gradients], z_rows, "pick_for_z")
-    rows, pieces = lax.optimization_barrier((z_hop(rows), pieces))
     kernel = functools.partial(pick_runs_kernel, (1, plane_cap, grid_z, 1))
-    rows = vmem_call(kernel, [rank_at], [rows], plane_rows, "pick_for_plane")
+    rows = vmem_call(kernel, [rank_at], [z_hop(rows)], plane_rows, "pick_for_plane")
+    rows, pieces = lax.optimization_barrier((rows, pieces))
     rows = plane_hop(rows)
     update = precondition_slot(here, core, rows, left_root, right_root, pieces)
     update = plane_hop(update).reshape((plane_rows,) + chunk)

time: 219 us -> 219 us (level)
    ppermute x3, waiting for transfers between devices: 41.1 us -> 4.9 us  [factor_pieces(): got.append(lax.ppermute(piece, ('core', 'x'), pairs))]
    all_to_all x1, waiting for transfers between devices: 0.01 us -> 34.3 us  [z_hop(): lax.all_to_all(rows, 'z', 0, 0, tiled=True).reshape((z_rows,) + chunk)]
  transfers between devices with their start and end apart: 6 -> 6, of which waited for: 4 -> 4; matrix products, arithmetic and copies ran while one was open for 0% -> 0% of each run, Pallas kernels for 1% -> 3%
where the time goes in v4:
time: 219 us; the launch traced here: 217 us
  waiting for transfers between devices  90.3 us (41%)
  blocking collectives  62.1 us (28%)
  starting transfers between devices  38.6 us (18%)
  Pallas kernels  20.9 us (10%)
  other arithmetic  3.3 us (2%)
    all_to_all x1, blocking collectives, z_hop(): lax.all_to_all(rows, 'z', 0, 0, tiled=True).reshape((z_rows,) + chunk)  62.1 us
    all_to_all x2, waiting for transfers between devices, plane_hop(): return lax.all_to_all(rows, plane_axes, 0, 0, tiled=True)  51 us
    all_to_all x1, waiting for transfers between devices, z_hop(): lax.all_to_all(rows, 'z', 0, 0, tiled=True).reshape((z_rows,) + chunk)  34.3 us
    all_to_all x1, starting transfers between devices, z_hop(): lax.all_to_all(rows, 'z', 0, 0, tiled=True).reshape((z_rows,) + chunk)  15.2 us
    all_to_all x2, starting transfers between devices, plane_hop(): return lax.all_to_all(rows, plane_axes, 0, 0, tiled=True)  14.2 us
    pallas_call x1, Pallas kernels, precondition_slot(): pl.pallas_call(slot_kernel, out_shape=jax.ShapeDtypeStruct(rows.shape, ro...  10.3 us
    ppermute x3, starting transfers between devices, factor_pieces(): got.append(lax.ppermute(piece, ('core', 'x'), pairs))  9.26 us
    pallas_call x5, Pallas kernels, vmem_call(): pl.pallas_call(kernel, out_shape=jax.ShapeDtypeStruct((count,) + arrays[0...  7.11 us
  transfers between devices with their start and end apart: 6, of which 4 were waited for; matrix products, arithmetic and copies ran while one was open for 0% of the time, Pallas kernels for 3%

profile of v4, /device:TPU:6, one launch (start us, length us, event | category | flops | bytes accessed | tf_op | source)
XLA Modules:
  0.0 216.7 jit_solution(2600871755256934582)
XLA Ops:
  0.6 0.7 and_select_fusion.42
  1.4 0.6 fusion.40
  2.7 213.9 %conditional.1 = (bf16[128,8,256]{2,1,0:T(8,128)(2,1)}, bf16[128,8,256]{2,1,0:T(8,128)(2,1)}) conditional(s32[]{:T(128)} %clamp.3, (s32[128]{0:T(128)}, bf16[128,8,256]{2,1,0:T(8,128)(2,1)}, bf16[3,256,1024]{2,1,0:T(8,128)(2,1)}, bf16[3,1024,256]{2,1,0:T(8,128)(2,1)}, bf16[128,8,256]{2,1,0:T(8,128)(2,1)}) %tuple.37, ...), branch_computations={%region_2.7_spmd, %region_7.12_spmd, %region_12.17_spmd, %region_1... | conditional | flops 4295227392 | bytes 58206448 | solution.py:324
  2.8 0.7 compare_select_fusion.16
  3.4 0.2 convert_reduce_fusion.2
  3.8 2.5 %pick_for_z.8 = bf16[240,8,256]{2,1,0:T(8,128)(2,1)} custom-call(s32[240]{0:T(256)S(1)} %select_reduce_fusion.6.index_ref, bf16[128,8,256]{2,1,0:T(8,128)(2,1)} %get-tuple-element.85.src_ref), custom_call_target="tpu_custom_call" | custom-call | tf_op jit(solution)/shard_map/cond/branch_2_fun/pick_for_z/pallas_call | solution.py:59
  6.2 15.2 %all-to-all-start.8 = ((bf16[16,15,8,256]{3,2,1,0:T(8,128)(2,1)}), bf16[16,15,8,256]{3,2,1,0:T(8,128)(2,1)S(1)}, u32[]{:S(2)}, u32[]{:S(2)}) async-start(bf16[16,15,8,256]{3,2,1,0:T(8,128)(2,1)} %bitcast.24), calls=%async_computation.8 | async-start | bytes 1966080 | tf_op jit(solution)/shard_map/cond/branch_2_fun/all_to_all | solution.py:296
  21.5 3.5 %pack_factors.8 = (bf16[512,1024]{1,0:T(8,128)(2,1)}, bf16[512,1024]{1,0:T(8,128)(2,1)S(1)}, bf16[512,1024]{1,0:T(8,128)(2,1)S(1)}) custom-call(s32[3]{0:T(128)S(1)} %pad_add_fusion.5.slot_ref, bf16[3,256,1024]{2,1,0:T(8,128)(2,1)} %get-tuple-element.86.left_ref.refs_1_, bf16[3,1024,256]{2,1,0:T(8,128)(2,1)} %get-tuple-element.87.right_ref.refs_2_), custom_call_target="tpu_custom_call" | custom-call | tf_op jit(solution)/shard_map/cond/branch_2_fun/pack_factors/pallas_call | solution.py:114
  25.0 1.3 collective-permute-start.6
  26.3 3.9 %collective-permute-start.7 = (bf16[512,1024]{1,0:T(8,128)(2,1)S(1)}, bf16[512,1024]{1,0:T(8,128)(2,1)}, u32[]{:S(2)}, u32[]{:S(2)}) collective-permute-start(bf16[512,1024]{1,0:T(8,128)(2,1)S(1)} %get-tuple-element.89), channel_id=1, source_target_pairs={{0,3},{1,0},{3,2},{4,7},{5,4},{6,5},{8,11},{9,8},{11,10},{12,15},{... | collective-permute-start | bytes 3145736 | tf_op jit(solution)/shard_map/cond/branch_2_fun/ppermute | solution.py:131
  30.2 4.1 %collective-permute-start.8 = (bf16[512,1024]{1,0:T(8,128)(2,1)S(1)}, bf16[512,1024]{1,0:T(8,128)(2,1)}, u32[]{:S(2)}, u32[]{:S(2)}) collective-permute-start(bf16[512,1024]{1,0:T(8,128)(2,1)S(1)} %get-tuple-element.90), channel_id=1, source_target_pairs={{1,2},{2,3},{3,0},{4,5},{6,7},{7,4},{9,10},{10,11},{11,8},{12,13},... | collective-permute-start | bytes 3145736 | tf_op jit(solution)/shard_map/cond/branch_2_fun/ppermute | solution.py:131
  34.4 34.3 %all-to-all-done.8 = bf16[16,15,8,256]{3,2,1,0:T(8,128)(2,1)S(1)} async-done(((bf16[16,15,8,256]{3,2,1,0:T(8,128)(2,1)}), bf16[16,15,8,256]{3,2,1,0:T(8,128)(2,1)S(1)}, u32[]{:S(2)}, u32[]{:S(2)}) %all-to-all-start.8) | async-done | bytes 983072 | tf_op jit(solution)/shard_map/cond/branch_2_fun/all_to_all | solution.py:296
  68.8 2.2 %pick_for_plane.8 = bf16[512,8,256]{2,1,0:T(8,128)(2,1)} custom-call(s32[32]{0:T(128)S(1)} %select_reduce_fusion.7.index_ref, bf16[240,8,256]{2,1,0:T(8,128)(2,1)S(1)} %bitcast.81), custom_call_target="tpu_custom_call" | custom-call | tf_op jit(solution)/shard_map/cond/branch_2_fun/pick_for_plane/pallas_call | solution.py:59
  70.9 4.9 %collective-permute-done.7.refs_4_ = bf16[512,1024]{1,0:T(8,128)(2,1)} collective-permute-done((bf16[512,1024]{1,0:T(8,128)(2,1)S(1)}, bf16[512,1024]{1,0:T(8,128)(2,1)}, u32[]{:S(2)}, u32[]{:S(2)}) %collective-permute-start.7) | collective-permute-done | bytes 1048608 | tf_op jit(solution)/shard_map/cond/branch_2_fun/ppermute | solution.py:131
  75.9 7.6 %all-to-all-start.9 = ((bf16[32,16,8,256]{3,2,1,0:T(8,128)(2,1)}), bf16[32,16,8,256]{3,2,1,0:T(8,128)(2,1)}, u32[]{:S(2)}, u32[]{:S(2)}) async-start(bf16[32,16,8,256]{3,2,1,0:T(8,128)(2,1)} %bitcast.29), calls=%async_computation.9 | async-start | bytes 4194304 | tf_op jit(solution)/shard_map/cond/branch_2_fun/all_to_all | solution.py:300
  83.5 0.6 pad_add_fusion.4.here_ref
  84.1 25.3 %all-to-all-done.9.refs_0_ = bf16[32,16,8,256]{3,2,1,0:T(8,128)(2,1)} async-done(((bf16[32,16,8,256]{3,2,1,0:T(8,128)(2,1)}), bf16[32,16,8,256]{3,2,1,0:T(8,128)(2,1)}, u32[]{:S(2)}, u32[]{:S(2)}) %all-to-all-start.9) | async-done | bytes 2097184 | tf_op jit(solution)/shard_map/cond/branch_2_fun/all_to_all | solution.py:300
  109.4 10.3 %precondition_slot.8 = bf16[32,16,8,256]{3,2,1,0:T(8,128)(2,1)} custom-call(s32[2]{0:T(128)} %pad_add_fusion.4.here_ref, bf16[32,16,8,256]{3,2,1,0:T(8,128)(2,1)} %all-to-all-done.9.refs_0_, bf16[3,256,1024]{2,1,0:T(8,128)(2,1)S(1)} %copy-done.2, bf16[3,1024,256]{2,1,0:T(8,128)(2,1)S(1)} %copy-done.8, bf16[512,1024]{1,0:T(8,128)(2,1)} %collective-permute-done.6.refs_3_, ...), custom_call_target="tpu_custom_call" | custom-call | flops 4294967296 | bytes 8388608 | tf_op jit(solution)/shard_map/cond/branch_2_fun/precondition_slot/pallas_call | solution.py:241
  119.7 6.5 %all-to-all-start.10 = ((bf16[32,16,8,256]{3,2,1,0:T(8,128)(2,1)}), bf16[32,16,8,256]{3,2,1,0:T(8,128)(2,1)S(1)}, u32[]{:S(2)}, u32[]{:S(2)}) async-start(bf16[32,16,8,256]{3,2,1,0:T(8,128)(2,1)} %precondition_slot.8), calls=%async_computation.10 | async-start | bytes 4194304 | tf_op jit(solution)/shard_map/cond/branch_2_fun/all_to_all | solution.py:300
  126.3 25.7 %all-to-all-done.10 = bf16[32,16,8,256]{3,2,1,0:T(8,128)(2,1)S(1)} async-done(((bf16[32,16,8,256]{3,2,1,0:T(8,128)(2,1)}), bf16[32,16,8,256]{3,2,1,0:T(8,128)(2,1)S(1)}, u32[]{:S(2)}, u32[]{:S(2)}) %all-to-all-start.10) | async-done | bytes 2097184 | tf_op jit(solution)/shard_map/cond/branch_2_fun/all_to_all | solution.py:300
  152.0 0.7 pick_back_for_z.8
  152.7 62.1 %all_to_all.98 = bf16[16,15,8,256]{3,2,1,0:T(8,128)(2,1)S(1)} all-to-all(bf16[16,15,8,256]{3,2,1,0:T(8,128)(2,1)S(1)} %bitcast.82), channel_id=1, replica_groups=mesh['y'=4,'z'=16,'core'=2,'x'=4] {'z'}, dimensions={0} | all-to-all | bytes 1966080 | tf_op jit(solution)/shard_map/cond/branch_2_fun/all_to_all | solution.py:296
  214.8 0.8 pick_step_rows.8.step_ref
  215.6 1.0 step.8
  (16 shorter events, 0.6 us)
Async XLA Ops:
  6.2 62.5 %all-to-all-start.8 = ((bf16[16,15,8,256]{3,2,1,0:T(8,128)(2,1)}), bf16[16,15,8,256]{3,2,1,0:T(8,128)(2,1)S(1)}, u32[]{:S(2)}, u32[]{:S(2)}) async-start(bf16[16,15,8,256]{3,2,1,0:T(8,128)(2,1)} %bitcast.24), calls=%async_computation.8 | async-start | bytes 1966080 | tf_op jit(solution)/shard_map/cond/branch_2_fun/all_to_all | solution.py:296
  25.0 45.9 %collective-permute-start.6 = (bf16[512,1024]{1,0:T(8,128)(2,1)}, bf16[512,1024]{1,0:T(8,128)(2,1)}, u32[]{:S(2)}, u32[]{:S(2)}) collective-permute-start(bf16[512,1024]{1,0:T(8,128)(2,1)} %get-tuple-element.88), channel_id=1, source_target_pairs={{0,2},{1,3},{2,0},{5,7},{6,4},{7,5},{8,10},{9,11},{10,8},{13,15},{... | collective-permute-start | bytes 3145736 | tf_op jit(solution)/shard_map/cond/branch_2_fun/ppermute | solution.py:131
  26.3 49.5 %collective-permute-start.7 = (bf16[512,1024]{1,0:T(8,128)(2,1)S(1)}, bf16[512,1024]{1,0:T(8,128)(2,1)}, u32[]{:S(2)}, u32[]{:S(2)}) collective-permute-start(bf16[512,1024]{1,0:T(8,128)(2,1)S(1)} %get-tuple-element.89), channel_id=1, source_target_pairs={{0,3},{1,0},{3,2},{4,7},{5,4},{6,5},{8,11},{9,8},{11,10},{12,15},{... | collective-permute-start | bytes 3145736 | tf_op jit(solution)/shard_map/cond/branch_2_fun/ppermute | solution.py:131
  30.2 45.7 %collective-permute-start.8 = (bf16[512,1024]{1,0:T(8,128)(2,1)S(1)}, bf16[512,1024]{1,0:T(8,128)(2,1)}, u32[]{:S(2)}, u32[]{:S(2)}) collective-permute-start(bf16[512,1024]{1,0:T(8,128)(2,1)S(1)} %get-tuple-element.90), channel_id=1, source_target_pairs={{1,2},{2,3},{3,0},{4,5},{6,7},{7,4},{9,10},{10,11},{11,8},{12,13},... | collective-permute-start | bytes 3145736 | tf_op jit(solution)/shard_map/cond/branch_2_fun/ppermute | solution.py:131
  75.8 33.5 %copy-start.2 = (bf16[3,256,1024]{2,1,0:T(8,128)(2,1)S(1)}, bf16[3,256,1024]{2,1,0:T(8,128)(2,1)}, u32[]{:S(2)}) copy-start(bf16[3,256,1024]{2,1,0:T(8,128)(2,1)} %get-tuple-element.86.left_ref.refs_1_) | copy-start | bytes 4718596 | tf_op jit(solution)/shard_map/cond
  75.8 33.5 %copy-start.8 = (bf16[3,1024,256]{2,1,0:T(8,128)(2,1)S(1)}, bf16[3,1024,256]{2,1,0:T(8,128)(2,1)}, u32[]{:S(2)}) copy-start(bf16[3,1024,256]{2,1,0:T(8,128)(2,1)} %get-tuple-element.87.right_ref.refs_2_) | copy-start | bytes 4718596 | tf_op jit(solution)/shard_map/cond
  75.9 33.5 %all-to-all-start.9 = ((bf16[32,16,8,256]{3,2,1,0:T(8,128)(2,1)}), bf16[32,16,8,256]{3,2,1,0:T(8,128)(2,1)}, u32[]{:S(2)}, u32[]{:S(2)}) async-start(bf16[32,16,8,256]{3,2,1,0:T(8,128)(2,1)} %bitcast.29), calls=%async_computation.9 | async-start | bytes 4194304 | tf_op jit(solution)/shard_map/cond/branch_2_fun/all_to_all | solution.py:300
  119.7 32.4 %all-to-all-start.10 = ((bf16[32,16,8,256]{3,2,1,0:T(8,128)(2,1)}), bf16[32,16,8,256]{3,2,1,0:T(8,128)(2,1)S(1)}, u32[]{:S(2)}, u32[]{:S(2)}) async-start(bf16[32,16,8,256]{3,2,1,0:T(8,128)(2,1)} %precondition_slot.8), calls=%async_computation.10 | async-start | bytes 4194304 | tf_op jit(solution)/shard_map/cond/branch_2_fun/all_to_all | solution.py:300
  152.7 62.9 %copy-start.20 = (bf16[128,8,256]{2,1,0:T(8,128)(2,1)S(1)}, bf16[128,8,256]{2,1,0:T(8,128)(2,1)}, u32[]{:S(2)}) copy-start(bf16[128,8,256]{2,1,0:T(8,128)(2,1)} %get-tuple-element.95.parameter_ref) | copy-start | bytes 1572868 | tf_op jit(solution)/shard_map/cond
  215.6 1.1 copy-start.14

commit v5 on v4

--- a/solution.py
+++ b/solution.py
@@ -138,9 +138,10 @@
 def slot_kernel(here_ref, *refs):
     arrived, own_left, own_right = refs[:3]
     pieces = refs[3 : 2 + grid_x]
-    out, left, right, rows, block, mixed, product, staged, sems = refs[2 + grid_x :]
+    out, left, right, rows, mixed, product, staged, sems = refs[2 + grid_x : -grid_x]
+    blocks = refs[-grid_x:]
     here, slot = here_ref[0], here_ref[1]
-    order = block.shape[0]
+    order = mixed.shape[0]
     share = order // grid_x
     row_local = rows.shape[2]
     pair = grid_core * row_local
@@ -168,10 +169,9 @@
     for copy in row_copies + left_copies + right_copies:
         copy.start()
 
-    def gather_tile(tile, total):
-        y, z = tile // grid_z, tile % grid_z
-        at = pl.ds(pl.multiple_of(tile * pair, pair), pair)
-        for x in range(grid_x):
+    def gather(x, y, total):
+        for z in range(grid_z):
+            at = pl.ds(pl.multiple_of(y * share + z * pair, pair), pair)
             both = jnp.concatenate(
                 [
                     rows[(y * grid_core + core) * grid_x + x, z].astype(jnp.float32)
@@ -180,26 +180,34 @@
                 axis=0,
             )
             total = total + both * both
-            block[at, x * share : (x + 1) * share] = both.astype(block.dtype)
+            blocks[x][at, :] = both.astype(jnp.bfloat16)
         return total
 
-    grad_sum = jnp.zeros((pair, share), jnp.float32)
-    for y in range(grid_y):
-        row_copies[y].wait()
-        grad_sum = lax.fori_loop(
-            y * grid_z, (y + 1) * grid_z, gather_tile, grad_sum, unroll=4
-        )
+    def mix(x, y):
+        to = pl.ds(pl.multiple_of(y * share, share), share)
+        mixed[to, x * share : (x + 1) * share] = jnp.dot(
+            left[y], blocks[x][...], preferred_element_type=jnp.float32
+        ).astype(mixed.dtype)
+
+    def mix_beside_gather(x, y, total):
+        mix(x, y)
+        return gather(x + 1, y, total)
+
+    for copy in row_copies:
+        copy.wait()
+    grad_sum = lax.fori_loop(
+        0, grid_y, functools.partial(gather, 0), jnp.zeros((pair, share), jnp.float32)
+    )
     for copy in left_copies:
         copy.wait()
-
-    def mix(tile, carry):
-        at = pl.ds(pl.multiple_of(tile * share, share), share)
-        mixed[:, at] = jnp.dot(
-            left[...].reshape(order, order), block[:, at], preferred_element_type=jnp.float32
-        ).astype(mixed.dtype)
-        return carry
-
-    lax.fori_loop(0, grid_x, mix, 0)
+    for x in range(grid_x - 1):
+        grad_sum = lax.fori_loop(0, grid_y, functools.partial(mix_beside_gather, x), grad_sum)
+
+    def mix_last(y, carry):
+        mix(grid_x - 1, y)
+        return carry
+
+    lax.fori_loop(0, grid_y, mix_last, 0)
     for copy in right_copies:
         copy.wait()
 
@@ -225,7 +233,7 @@
 
     out_copies = []
     for y, span in enumerate(spans):
-        lax.fori_loop(y * grid_z, (y + 1) * grid_z, scatter_tile, 0, unroll=4)
+        lax.fori_loop(y * grid_z, (y + 1) * grid_z, scatter_tile, 0)
         out_copies.append(
             pltpu.make_async_copy(staged.at[span], out.at[span], sems.at[last_sem + y])
         )
@@ -248,11 +256,11 @@
             pltpu.VMEM((grid_x, order, share), jnp.bfloat16),
             pltpu.VMEM(rows.shape, rows.dtype),
             pltpu.VMEM((order, order), jnp.bfloat16),
-            pltpu.VMEM((order, order), jnp.bfloat16),
             pltpu.VMEM((grid_x, order, share), jnp.float32),
             pltpu.VMEM(rows.shape, rows.dtype),
             pltpu.SemaphoreType.DMA((last_sem + 2 * grid_y,)),
-        ],
+        ]
+        + [pltpu.VMEM((order, share), jnp.bfloat16)] * grid_x,
         compiler_params=pltpu.CompilerParams(vmem_limit_bytes=60 * 1024 * 1024),
         cost_estimate=pl.CostEstimate(
             flops=4 * order**3, bytes_accessed=8 * order * order, transcendentals=0

time: 219 us -> 219 us (level)
  no operation moved by 1% of the time
where the time goes in v5:
time: 219 us
  waiting for transfers between devices  90.3 us (41%)
  blocking collectives  62.1 us (28%)
  starting transfers between devices  38.6 us (18%)
  Pallas kernels  23 us (11%)
  other arithmetic  3.3 us (2%)
    all_to_all x1, blocking collectives, z_hop(): lax.all_to_all(rows, 'z', 0, 0, tiled=True).reshape((z_rows,) + chunk)  62.1 us
    all_to_all x2, waiting for transfers between devices, plane_hop(): return lax.all_to_all(rows, plane_axes, 0, 0, tiled=True)  51 us
    all_to_all x1, waiting for transfers between devices, z_hop(): lax.all_to_all(rows, 'z', 0, 0, tiled=True).reshape((z_rows,) + chunk)  34.3 us
    all_to_all x1, starting transfers between devices, z_hop(): lax.all_to_all(rows, 'z', 0, 0, tiled=True).reshape((z_rows,) + chunk)  15.2 us
    all_to_all x2, starting transfers between devices, plane_hop(): return lax.all_to_all(rows, plane_axes, 0, 0, tiled=True)  14.2 us
    pallas_call x1, Pallas kernels, precondition_slot(): pl.pallas_call(slot_kernel, out_shape=jax.ShapeDtypeStruct(rows.shape, ro...  12.4 us
    ppermute x3, starting transfers between devices, factor_pieces(): got.append(lax.ppermute(piece, ('core', 'x'), pairs))  9.26 us
    pallas_call x5, Pallas kernels, vmem_call(): pl.pallas_call(kernel, out_shape=jax.ShapeDtypeStruct((count,) + arrays[0...  7.11 us
  transfers between devices with their start and end apart: 6, of which 4 were waited for; matrix products, arithmetic and copies ran while one was open for 0% of the time, Pallas kernels for 3%

profile of v5, /device:TPU:6, one launch (start us, length us, event | category | flops | bytes accessed | tf_op | source)
XLA Modules:
  0.0 218.8 jit_solution(4192667925052600017)
XLA Ops:
  0.6 0.7 and_select_fusion.42
  1.4 0.6 fusion.40
  2.7 216.1 %conditional.1 = (bf16[128,8,256]{2,1,0:T(8,128)(2,1)}, bf16[128,8,256]{2,1,0:T(8,128)(2,1)}) conditional(s32[]{:T(128)} %clamp.3, (s32[128]{0:T(128)}, bf16[128,8,256]{2,1,0:T(8,128)(2,1)}, bf16[3,256,1024]{2,1,0:T(8,128)(2,1)}, bf16[3,1024,256]{2,1,0:T(8,128)(2,1)}, bf16[128,8,256]{2,1,0:T(8,128)(2,1)}) %tuple.37, ...), branch_computations={%region_2.7_spmd, %region_7.12_spmd, %region_12.17_spmd, %region_1... | conditional | flops 4295227392 | bytes 58206448 | solution.py:332
  2.8 0.7 compare_select_fusion.16
  3.4 0.2 convert_reduce_fusion.2
  3.8 2.5 %pick_for_z.8 = bf16[240,8,256]{2,1,0:T(8,128)(2,1)} custom-call(s32[240]{0:T(256)S(1)} %select_reduce_fusion.6.index_ref, bf16[128,8,256]{2,1,0:T(8,128)(2,1)} %get-tuple-element.85.src_ref), custom_call_target="tpu_custom_call" | custom-call | tf_op jit(solution)/shard_map/cond/branch_2_fun/pick_for_z/pallas_call | solution.py:59
  6.2 15.2 %all-to-all-start.8 = ((bf16[16,15,8,256]{3,2,1,0:T(8,128)(2,1)}), bf16[16,15,8,256]{3,2,1,0:T(8,128)(2,1)S(1)}, u32[]{:S(2)}, u32[]{:S(2)}) async-start(bf16[16,15,8,256]{3,2,1,0:T(8,128)(2,1)} %bitcast.24), calls=%async_computation.8 | async-start | bytes 1966080 | tf_op jit(solution)/shard_map/cond/branch_2_fun/all_to_all | solution.py:304
  21.5 3.5 %pack_factors.8 = (bf16[512,1024]{1,0:T(8,128)(2,1)}, bf16[512,1024]{1,0:T(8,128)(2,1)S(1)}, bf16[512,1024]{1,0:T(8,128)(2,1)S(1)}) custom-call(s32[3]{0:T(128)S(1)} %pad_add_fusion.5.slot_ref, bf16[3,256,1024]{2,1,0:T(8,128)(2,1)} %get-tuple-element.86.left_ref.refs_1_, bf16[3,1024,256]{2,1,0:T(8,128)(2,1)} %get-tuple-element.87.right_ref.refs_2_), custom_call_target="tpu_custom_call" | custom-call | tf_op jit(solution)/shard_map/cond/branch_2_fun/pack_factors/pallas_call | solution.py:114
  25.0 1.3 collective-permute-start.6
  26.3 3.9 %collective-permute-start.7 = (bf16[512,1024]{1,0:T(8,128)(2,1)S(1)}, bf16[512,1024]{1,0:T(8,128)(2,1)}, u32[]{:S(2)}, u32[]{:S(2)}) collective-permute-start(bf16[512,1024]{1,0:T(8,128)(2,1)S(1)} %get-tuple-element.89), channel_id=1, source_target_pairs={{0,3},{1,0},{3,2},{4,7},{5,4},{6,5},{8,11},{9,8},{11,10},{12,15},{... | collective-permute-start | bytes 3145736 | tf_op jit(solution)/shard_map/cond/branch_2_fun/ppermute | solution.py:131
  30.2 4.1 %collective-permute-start.8 = (bf16[512,1024]{1,0:T(8,128)(2,1)S(1)}, bf16[512,1024]{1,0:T(8,128)(2,1)}, u32[]{:S(2)}, u32[]{:S(2)}) collective-permute-start(bf16[512,1024]{1,0:T(8,128)(2,1)S(1)} %get-tuple-element.90), channel_id=1, source_target_pairs={{1,2},{2,3},{3,0},{4,5},{6,7},{7,4},{9,10},{10,11},{11,8},{12,13},... | collective-permute-start | bytes 3145736 | tf_op jit(solution)/shard_map/cond/branch_2_fun/ppermute | solution.py:131
  34.4 34.3 %all-to-all-done.8 = bf16[16,15,8,256]{3,2,1,0:T(8,128)(2,1)S(1)} async-done(((bf16[16,15,8,256]{3,2,1,0:T(8,128)(2,1)}), bf16[16,15,8,256]{3,2,1,0:T(8,128)(2,1)S(1)}, u32[]{:S(2)}, u32[]{:S(2)}) %all-to-all-start.8) | async-done | bytes 983072 | tf_op jit(solution)/shard_map/cond/branch_2_fun/all_to_all | solution.py:304
  68.8 2.2 pick_for_plane.8
  70.9 4.9 %collective-permute-done.7.refs_4_ = bf16[512,1024]{1,0:T(8,128)(2,1)} collective-permute-done((bf16[512,1024]{1,0:T(8,128)(2,1)S(1)}, bf16[512,1024]{1,0:T(8,128)(2,1)}, u32[]{:S(2)}, u32[]{:S(2)}) %collective-permute-start.7) | collective-permute-done | bytes 1048608 | tf_op jit(solution)/shard_map/cond/branch_2_fun/ppermute | solution.py:131
  75.9 7.6 %all-to-all-start.9 = ((bf16[32,16,8,256]{3,2,1,0:T(8,128)(2,1)}), bf16[32,16,8,256]{3,2,1,0:T(8,128)(2,1)}, u32[]{:S(2)}, u32[]{:S(2)}) async-start(bf16[32,16,8,256]{3,2,1,0:T(8,128)(2,1)} %bitcast.29), calls=%async_computation.9 | async-start | bytes 4194304 | tf_op jit(solution)/shard_map/cond/branch_2_fun/all_to_all | solution.py:308
  83.5 0.6 pad_add_fusion.4.here_ref
  84.1 25.3 %all-to-all-done.9.refs_0_ = bf16[32,16,8,256]{3,2,1,0:T(8,128)(2,1)} async-done(((bf16[32,16,8,256]{3,2,1,0:T(8,128)(2,1)}), bf16[32,16,8,256]{3,2,1,0:T(8,128)(2,1)}, u32[]{:S(2)}, u32[]{:S(2)}) %all-to-all-start.9) | async-done | bytes 2097184 | tf_op jit(solution)/shard_map/cond/branch_2_fun/all_to_all | solution.py:308
  109.4 12.4 %precondition_slot.8 = bf16[32,16,8,256]{3,2,1,0:T(8,128)(2,1)} custom-call(s32[2]{0:T(128)} %pad_add_fusion.4.here_ref, bf16[32,16,8,256]{3,2,1,0:T(8,128)(2,1)} %all-to-all-done.9.refs_0_, bf16[3,256,1024]{2,1,0:T(8,128)(2,1)S(1)} %copy-done.2, bf16[3,1024,256]{2,1,0:T(8,128)(2,1)S(1)} %copy-done.8, bf16[512,1024]{1,0:T(8,128)(2,1)} %collective-permute-done.6.refs_3_, ...), custom_call_target="tpu_custom_call" | custom-call | flops 4294967296 | bytes 8388608 | tf_op jit(solution)/shard_map/cond/branch_2_fun/precondition_slot/pallas_call | solution.py:249
  121.8 6.5 %all-to-all-start.10 = ((bf16[32,16,8,256]{3,2,1,0:T(8,128)(2,1)}), bf16[32,16,8,256]{3,2,1,0:T(8,128)(2,1)S(1)}, u32[]{:S(2)}, u32[]{:S(2)}) async-start(bf16[32,16,8,256]{3,2,1,0:T(8,128)(2,1)} %precondition_slot.8), calls=%async_computation.10 | async-start | bytes 4194304 | tf_op jit(solution)/shard_map/cond/branch_2_fun/all_to_all | solution.py:308
  128.5 25.7 %all-to-all-done.10 = bf16[32,16,8,256]{3,2,1,0:T(8,128)(2,1)S(1)} async-done(((bf16[32,16,8,256]{3,2,1,0:T(8,128)(2,1)}), bf16[32,16,8,256]{3,2,1,0:T(8,128)(2,1)S(1)}, u32[]{:S(2)}, u32[]{:S(2)}) %all-to-all-start.10) | async-done | bytes 2097184 | tf_op jit(solution)/shard_map/cond/branch_2_fun/all_to_all | solution.py:308
  154.2 0.7 pick_back_for_z.8
  154.9 62.1 %all_to_all.98 = bf16[16,15,8,256]{3,2,1,0:T(8,128)(2,1)S(1)} all-to-all(bf16[16,15,8,256]{3,2,1,0:T(8,128)(2,1)S(1)} %bitcast.82), channel_id=1, replica_groups=mesh['y'=4,'z'=16,'core'=2,'x'=4] {'z'}, dimensions={0} | all-to-all | bytes 1966080 | tf_op jit(solution)/shard_map/cond/branch_2_fun/all_to_all | solution.py:304
  217.0 0.8 pick_step_rows.8.step_ref
  217.8 1.0 step.8
  (16 shorter events, 0.6 us)
Async XLA Ops:
  6.2 62.5 %all-to-all-start.8 = ((bf16[16,15,8,256]{3,2,1,0:T(8,128)(2,1)}), bf16[16,15,8,256]{3,2,1,0:T(8,128)(2,1)S(1)}, u32[]{:S(2)}, u32[]{:S(2)}) async-start(bf16[16,15,8,256]{3,2,1,0:T(8,128)(2,1)} %bitcast.24), calls=%async_computation.8 | async-start | bytes 1966080 | tf_op jit(solution)/shard_map/cond/branch_2_fun/all_to_all | solution.py:304
  25.0 45.9 %collective-permute-start.6 = (bf16[512,1024]{1,0:T(8,128)(2,1)}, bf16[512,1024]{1,0:T(8,128)(2,1)}, u32[]{:S(2)}, u32[]{:S(2)}) collective-permute-start(bf16[512,1024]{1,0:T(8,128)(2,1)} %get-tuple-element.88), channel_id=1, source_target_pairs={{0,2},{1,3},{2,0},{5,7},{6,4},{7,5},{8,10},{9,11},{10,8},{13,15},{... | collective-permute-start | bytes 3145736 | tf_op jit(solution)/shard_map/cond/branch_2_fun/ppermute | solution.py:131
  26.3 49.5 %collective-permute-start.7 = (bf16[512,1024]{1,0:T(8,128)(2,1)S(1)}, bf16[512,1024]{1,0:T(8,128)(2,1)}, u32[]{:S(2)}, u32[]{:S(2)}) collective-permute-start(bf16[512,1024]{1,0:T(8,128)(2,1)S(1)} %get-tuple-element.89), channel_id=1, source_target_pairs={{0,3},{1,0},{3,2},{4,7},{5,4},{6,5},{8,11},{9,8},{11,10},{12,15},{... | collective-permute-start | bytes 3145736 | tf_op jit(solution)/shard_map/cond/branch_2_fun/ppermute | solution.py:131
  30.2 45.7 %collective-permute-start.8 = (bf16[512,1024]{1,0:T(8,128)(2,1)S(1)}, bf16[512,1024]{1,0:T(8,128)(2,1)}, u32[]{:S(2)}, u32[]{:S(2)}) collective-permute-start(bf16[512,1024]{1,0:T(8,128)(2,1)S(1)} %get-tuple-element.90), channel_id=1, source_target_pairs={{1,2},{2,3},{3,0},{4,5},{6,7},{7,4},{9,10},{10,11},{11,8},{12,13},... | collective-permute-start | bytes 3145736 | tf_op jit(solution)/shard_map/cond/branch_2_fun/ppermute | solution.py:131
  75.8 33.5 %copy-start.2 = (bf16[3,256,1024]{2,1,0:T(8,128)(2,1)S(1)}, bf16[3,256,1024]{2,1,0:T(8,128)(2,1)}, u32[]{:S(2)}) copy-start(bf16[3,256,1024]{2,1,0:T(8,128)(2,1)} %get-tuple-element.86.left_ref.refs_1_) | copy-start | bytes 4718596 | tf_op jit(solution)/shard_map/cond
  75.8 33.5 %copy-start.8 = (bf16[3,1024,256]{2,1,0:T(8,128)(2,1)S(1)}, bf16[3,1024,256]{2,1,0:T(8,128)(2,1)}, u32[]{:S(2)}) copy-start(bf16[3,1024,256]{2,1,0:T(8,128)(2,1)} %get-tuple-element.87.right_ref.refs_2_) | copy-start | bytes 4718596 | tf_op jit(solution)/shard_map/cond
  75.9 33.5 %all-to-all-start.9 = ((bf16[32,16,8,256]{3,2,1,0:T(8,128)(2,1)}), bf16[32,16,8,256]{3,2,1,0:T(8,128)(2,1)}, u32[]{:S(2)}, u32[]{:S(2)}) async-start(bf16[32,16,8,256]{3,2,1,0:T(8,128)(2,1)} %bitcast.29), calls=%async_computation.9 | async-start | bytes 4194304 | tf_op jit(solution)/shard_map/cond/branch_2_fun/all_to_all | solution.py:308
  121.8 32.4 %all-to-all-start.10 = ((bf16[32,16,8,256]{3,2,1,0:T(8,128)(2,1)}), bf16[32,16,8,256]{3,2,1,0:T(8,128)(2,1)S(1)}, u32[]{:S(2)}, u32[]{:S(2)}) async-start(bf16[32,16,8,256]{3,2,1,0:T(8,128)(2,1)} %precondition_slot.8), calls=%async_computation.10 | async-start | bytes 4194304 | tf_op jit(solution)/shard_map/cond/branch_2_fun/all_to_all | solution.py:308
  154.9 62.9 %copy-start.20 = (bf16[128,8,256]{2,1,0:T(8,128)(2,1)S(1)}, bf16[128,8,256]{2,1,0:T(8,128)(2,1)}, u32[]{:S(2)}) copy-start(bf16[128,8,256]{2,1,0:T(8,128)(2,1)} %get-tuple-element.95.parameter_ref) | copy-start | bytes 1572868 | tf_op jit(solution)/shard_map/cond
  217.7 1.1 copy-start.14

commit v6 on v4

--- a/solution.py
+++ b/solution.py
@@ -13,6 +13,16 @@
 plane_axes = ("y", "core", "x")
 fsdp_axes = ("y", "z", "core")
 plane_devices = grid_y * grid_core * grid_x
+
+
+def z_place(z, core):
+    return ((7 + 2 * core) * z) % grid_z
+
+
+z_groups = [
+    [z_place(place, core) * grid_core + core for place in range(grid_z)]
+    for core in range(grid_core)
+]
 plane_capacities = (13, 14, 15, 16, 18, 24)
 
 pick_run = 8
@@ -29,13 +39,15 @@
     lax.fori_loop(0, out_ref.shape[0] // pick_run, some, 0)
 
 
-def pick_runs_kernel(strides, index_ref, src_ref, out_ref):
+def pick_runs_kernel(strides, z_in_source, index_ref, z_ref, src_ref, out_ref):
     src_run, src_step, out_run, out_step = strides
+    z_at = [z_ref[place] for place in range(grid_z)]
 
     def one(at, carry):
         src_at, out_at = index_ref[at] * src_run, at * out_run
-        for z in range(grid_z):
-            out_ref[out_at + z * out_step] = src_ref[src_at + z * src_step]
+        for place in range(grid_z):
+            a, b = (z_at[place], place) if z_in_source else (place, z_at[place])
+            out_ref[out_at + b * out_step] = src_ref[src_at + a * src_step]
         return carry
 
     lax.fori_loop(0, index_ref.shape[0], one, 0)
@@ -283,8 +295,9 @@
     ids = jnp.arange(block_count, dtype=jnp.int32)
     earlier = (plane[:, None] == plane[None, :]) & (ids[None, :] < ids[:, None])
     rank = jnp.sum(earlier.astype(jnp.int32), axis=1)
-    place_of = plane * plane_cap + rank
+    place_of = z_place(plane, core) * plane_cap + rank
     my_z = lax.axis_index("z")
+    z_at = z_place(jnp.arange(grid_z, dtype=jnp.int32), core)
     block_at = place(ids, place_of, grid_z * plane_cap)
     mine = plane == my_z
     rank_at = place(rank, jnp.where(mine, in_plane, plane_devices), plane_devices)
@@ -293,21 +306,24 @@
 
     def z_hop(rows):
         rows = rows.reshape((grid_z, plane_cap) + chunk)
-        return lax.all_to_all(rows, "z", 0, 0, tiled=True).reshape((z_rows,) + chunk)
+        rows = lax.all_to_all(
+            rows, ("z", "core"), 0, 0, axis_index_groups=z_groups, tiled=True
+        )
+        return rows.reshape((z_rows,) + chunk)
 
     def plane_hop(rows):
         rows = rows.reshape((plane_devices, grid_z) + chunk)
         return lax.all_to_all(rows, plane_axes, 0, 0, tiled=True)
 
     rows = vmem_call(pick_kernel, [block_at], [gradients], z_rows, "pick_for_z")
-    kernel = functools.partial(pick_runs_kernel, (1, plane_cap, grid_z, 1))
-    rows = vmem_call(kernel, [rank_at], [z_hop(rows)], plane_rows, "pick_for_plane")
+    kernel = functools.partial(pick_runs_kernel, (1, plane_cap, grid_z, 1), False)
+    rows = vmem_call(kernel, [rank_at, z_at], [z_hop(rows)], plane_rows, "pick_for_plane")
     rows, pieces = lax.optimization_barrier((rows, pieces))
     rows = plane_hop(rows)
     update = precondition_slot(here, core, rows, left_root, right_root, pieces)
     update = plane_hop(update).reshape((plane_rows,) + chunk)
-    kernel = functools.partial(pick_runs_kernel, (grid_z, 1, 1, plane_cap))
-    update = vmem_call(kernel, [holder_at], [update], z_rows, "pick_back_for_z")
+    kernel = functools.partial(pick_runs_kernel, (grid_z, 1, 1, plane_cap), True)
+    update = vmem_call(kernel, [holder_at, z_at], [update], z_rows, "pick_back_for_z")
     update = z_hop(update)
     step_rows = vmem_call(pick_kernel, [place_of], [update], block_count, "pick_step_rows")
     new_params = vmem_call(step_kernel, [], [step_rows, parameters], block_count, "step")

time: 219 us -> 222 us (1.014)
  the two profiles are of different devices: /device:TPU:6 before, /device:TPU:36 now
where the time goes in v6:
time: 222 us
  waiting for transfers between devices  91.3 us (41%)
  blocking collectives  66.1 us (30%)
  starting transfers between devices  37.4 us (17%)
  Pallas kernels  21.9 us (10%)
  other arithmetic  3.34 us (2%)
    all_to_all x1, blocking collectives, z_hop(): lax.all_to_all(rows, ('z', 'core'), 0, 0, axis_index_groups=z_groups, til...  66.1 us
    all_to_all x2, waiting for transfers between devices, plane_hop(): return lax.all_to_all(rows, plane_axes, 0, 0, tiled=True)  52.5 us
    all_to_all x1, waiting for transfers between devices, z_hop(): lax.all_to_all(rows, ('z', 'core'), 0, 0, axis_index_groups=z_groups, til...  38.8 us
    all_to_all x1, starting transfers between devices, z_hop(): lax.all_to_all(rows, ('z', 'core'), 0, 0, axis_index_groups=z_groups, til...  15.2 us
    all_to_all x2, starting transfers between devices, plane_hop(): return lax.all_to_all(rows, plane_axes, 0, 0, tiled=True)  14 us
    pallas_call x1, Pallas kernels, precondition_slot(): pl.pallas_call(slot_kernel, out_shape=jax.ShapeDtypeStruct(rows.shape, ro...  10.3 us
    ppermute x3, starting transfers between devices, factor_pieces(): got.append(lax.ppermute(piece, ('core', 'x'), pairs))  8.24 us
    pallas_call x5, Pallas kernels, vmem_call(): pl.pallas_call(kernel, out_shape=jax.ShapeDtypeStruct((count,) + arrays[0...  7.82 us
  transfers between devices with their start and end apart: 6, of which 3 were waited for; matrix products, arithmetic and copies ran while one was open for 0% of the time, Pallas kernels for 3%

profile of v6, /device:TPU:36, one launch (start us, length us, event | category | flops | bytes accessed | tf_op | source)
XLA Modules:
  0.0 221.8 jit_solution(7318011870094061778)
XLA Ops:
  0.6 0.7 and_select_fusion.54
  1.4 0.6 fusion.64
  2.7 219.1 %conditional.1 = (bf16[128,8,256]{2,1,0:T(8,128)(2,1)}, bf16[128,8,256]{2,1,0:T(8,128)(2,1)}) conditional(s32[]{:T(128)} %clamp.3, (s32[128]{0:T(128)}, bf16[128,8,256]{2,1,0:T(8,128)(2,1)}, bf16[3,256,1024]{2,1,0:T(8,128)(2,1)}, bf16[3,1024,256]{2,1,0:T(8,128)(2,1)}, bf16[128,8,256]{2,1,0:T(8,128)(2,1)}) %tuple.37, ...), branch_computations={%region_2.7_spmd, %region_7.12_spmd, %region_12.17_spmd, %region_1... | conditional | flops 4295228928 | bytes 51915060 | solution.py:340
  2.9 0.7 compare_select_fusion.38
  3.6 0.2 convert_reduce_fusion.3
  3.8 0.1 select_reduce_fusion.9.index_ref
  3.9 2.5 %pick_for_z.9 = bf16[256,8,256]{2,1,0:T(8,128)(2,1)} custom-call(s32[256]{0:T(256)S(1)} %select_reduce_fusion.9.index_ref, bf16[128,8,256]{2,1,0:T(8,128)(2,1)} %get-tuple-element.97.src_ref), custom_call_target="tpu_custom_call" | custom-call | tf_op jit(solution)/shard_map/cond/branch_3_fun/pick_for_z/pallas_call | solution.py:71
  6.4 15.2 %all-to-all-start.12 = ((bf16[16,16,8,256]{3,2,1,0:T(8,128)(2,1)}), bf16[16,16,8,256]{3,2,1,0:T(8,128)(2,1)S(1)}, u32[]{:S(2)}, u32[]{:S(2)}) async-start(bf16[16,16,8,256]{3,2,1,0:T(8,128)(2,1)} %bitcast.35), calls=%async_computation.12 | async-start | bytes 2097152 | tf_op jit(solution)/shard_map/cond/branch_3_fun/all_to_all | solution.py:309
  21.7 3.8 %pack_factors.9 = (bf16[512,1024]{1,0:T(8,128)(2,1)}, bf16[512,1024]{1,0:T(8,128)(2,1)}, bf16[512,1024]{1,0:T(8,128)(2,1)S(1)}) custom-call(s32[3]{0:T(128)S(1)} %pad_add_fusion.7.slot_ref, bf16[3,256,1024]{2,1,0:T(8,128)(2,1)} %get-tuple-element.98.left_ref.refs_1_, bf16[3,1024,256]{2,1,0:T(8,128)(2,1)} %get-tuple-element.99.right_ref.refs_2_), custom_call_target="tpu_custom_call" | custom-call | tf_op jit(solution)/shard_map/cond/branch_3_fun/pack_factors/pallas_call | solution.py:126
  25.6 2.4 %collective-permute-start.9 = (bf16[512,1024]{1,0:T(8,128)(2,1)}, bf16[512,1024]{1,0:T(8,128)(2,1)}, u32[]{:S(2)}, u32[]{:S(2)}) collective-permute-start(bf16[512,1024]{1,0:T(8,128)(2,1)} %get-tuple-element.100), channel_id=1, source_target_pairs={{0,2},{1,3},{2,0},{5,7},{6,4},{7,5},{8,10},{9,11},{10,8},{13,15},{... | collective-permute-start | bytes 3145736 | tf_op jit(solution)/shard_map/cond/branch_3_fun/ppermute | solution.py:143
  28.0 1.3 collective-permute-start.10
  29.3 4.6 %collective-permute-start.11 = (bf16[512,1024]{1,0:T(8,128)(2,1)S(1)}, bf16[512,1024]{1,0:T(8,128)(2,1)}, u32[]{:S(2)}, u32[]{:S(2)}) collective-permute-start(bf16[512,1024]{1,0:T(8,128)(2,1)S(1)} %get-tuple-element.102), channel_id=1, source_target_pairs={{1,2},{2,3},{3,0},{4,5},{6,7},{7,4},{9,10},{10,11},{11,8},{12,13},... | collective-permute-start | bytes 3145736 | tf_op jit(solution)/shard_map/cond/branch_3_fun/ppermute | solution.py:143
  34.0 38.8 %all-to-all-done.12 = bf16[16,16,8,256]{3,2,1,0:T(8,128)(2,1)S(1)} async-done(((bf16[16,16,8,256]{3,2,1,0:T(8,128)(2,1)}), bf16[16,16,8,256]{3,2,1,0:T(8,128)(2,1)S(1)}, u32[]{:S(2)}, u32[]{:S(2)}) %all-to-all-start.12) | async-done | bytes 1048608 | tf_op jit(solution)/shard_map/cond/branch_3_fun/all_to_all | solution.py:309
  72.7 2.6 %pick_for_plane.9 = bf16[512,8,256]{2,1,0:T(8,128)(2,1)} custom-call(s32[32]{0:T(128)S(1)} %select_reduce_fusion.10.index_ref, s32[16]{0:T(128)S(1)} %and_select_fusion.27.z_ref, bf16[256,8,256]{2,1,0:T(8,128)(2,1)S(1)} %bitcast.78), custom_call_target="tpu_custom_call" | custom-call | tf_op jit(solution)/shard_map/cond/branch_3_fun/pick_for_plane/pallas_call | solution.py:71
  75.4 8.2 %all-to-all-start.13 = ((bf16[32,16,8,256]{3,2,1,0:T(8,128)(2,1)}), bf16[32,16,8,256]{3,2,1,0:T(8,128)(2,1)}, u32[]{:S(2)}, u32[]{:S(2)}) async-start(bf16[32,16,8,256]{3,2,1,0:T(8,128)(2,1)} %bitcast.40), calls=%async_computation.13 | async-start | bytes 4194304 | tf_op jit(solution)/shard_map/cond/branch_3_fun/all_to_all | solution.py:316
  83.6 0.6 pad_add_fusion.6.here_ref
  84.2 26.0 %all-to-all-done.13.refs_0_ = bf16[32,16,8,256]{3,2,1,0:T(8,128)(2,1)} async-done(((bf16[32,16,8,256]{3,2,1,0:T(8,128)(2,1)}), bf16[32,16,8,256]{3,2,1,0:T(8,128)(2,1)}, u32[]{:S(2)}, u32[]{:S(2)}) %all-to-all-start.13) | async-done | bytes 2097184 | tf_op jit(solution)/shard_map/cond/branch_3_fun/all_to_all | solution.py:316
  110.3 10.3 %precondition_slot.9 = bf16[32,16,8,256]{3,2,1,0:T(8,128)(2,1)} custom-call(s32[2]{0:T(128)} %pad_add_fusion.6.here_ref, bf16[32,16,8,256]{3,2,1,0:T(8,128)(2,1)} %all-to-all-done.13.refs_0_, bf16[3,256,1024]{2,1,0:T(8,128)(2,1)S(1)} %copy-done.3, bf16[3,1024,256]{2,1,0:T(8,128)(2,1)} %get-tuple-element.99.right_ref.refs_2_, ...), custom_call_target="tpu_custom_call" | custom-call | flops 4294967296 | bytes 8388608 | tf_op jit(solution)/shard_map/cond/branch_3_fun/precondition_slot/pallas_call | solution.py:253
  120.6 5.8 %all-to-all-start.14 = ((bf16[32,16,8,256]{3,2,1,0:T(8,128)(2,1)}), bf16[32,16,8,256]{3,2,1,0:T(8,128)(2,1)S(1)}, u32[]{:S(2)}, u32[]{:S(2)}) async-start(bf16[32,16,8,256]{3,2,1,0:T(8,128)(2,1)} %precondition_slot.9), calls=%async_computation.14 | async-start | bytes 4194304 | tf_op jit(solution)/shard_map/cond/branch_3_fun/all_to_all | solution.py:316
  126.5 26.5 %all-to-all-done.14 = bf16[32,16,8,256]{3,2,1,0:T(8,128)(2,1)S(1)} async-done(((bf16[32,16,8,256]{3,2,1,0:T(8,128)(2,1)}), bf16[32,16,8,256]{3,2,1,0:T(8,128)(2,1)S(1)}, u32[]{:S(2)}, u32[]{:S(2)}) %all-to-all-start.14) | async-done | bytes 2097184 | tf_op jit(solution)/shard_map/cond/branch_3_fun/all_to_all | solution.py:316
  153.0 0.9 pick_back_for_z.9
  153.9 66.1 %all_to_all.99 = bf16[16,16,8,256]{3,2,1,0:T(8,128)(2,1)S(1)} all-to-all(bf16[16,16,8,256]{3,2,1,0:T(8,128)(2,1)S(1)} %bitcast.79), channel_id=1, replica_groups={{0,56,112,40,96,24,80,8,64,120,48,104,32,88,16,72},{4,76,20,92,36,108,5..., dimensions={0} | all-to-all | bytes 2097152 | tf_op jit(solution)/shard_map/cond/branch_3_fun/all_to_all | solution.py:309
  220.0 0.8 pick_step_rows.9.step_ref
  220.8 1.0 step.9
  (15 shorter events, 0.5 us)
Async XLA Ops:
  6.4 66.3 %all-to-all-start.12 = ((bf16[16,16,8,256]{3,2,1,0:T(8,128)(2,1)}), bf16[16,16,8,256]{3,2,1,0:T(8,128)(2,1)S(1)}, u32[]{:S(2)}, u32[]{:S(2)}) async-start(bf16[16,16,8,256]{3,2,1,0:T(8,128)(2,1)} %bitcast.35), calls=%async_computation.12 | async-start | bytes 2097152 | tf_op jit(solution)/shard_map/cond/branch_3_fun/all_to_all | solution.py:309
  25.6 49.8 %collective-permute-start.9 = (bf16[512,1024]{1,0:T(8,128)(2,1)}, bf16[512,1024]{1,0:T(8,128)(2,1)}, u32[]{:S(2)}, u32[]{:S(2)}) collective-permute-start(bf16[512,1024]{1,0:T(8,128)(2,1)} %get-tuple-element.100), channel_id=1, source_target_pairs={{0,2},{1,3},{2,0},{5,7},{6,4},{7,5},{8,10},{9,11},{10,8},{13,15},{... | collective-permute-start | bytes 3145736 | tf_op jit(solution)/shard_map/cond/branch_3_fun/ppermute | solution.py:143
  28.0 47.4 %collective-permute-start.10 = (bf16[512,1024]{1,0:T(8,128)(2,1)}, bf16[512,1024]{1,0:T(8,128)(2,1)}, u32[]{:S(2)}, u32[]{:S(2)}) collective-permute-start(bf16[512,1024]{1,0:T(8,128)(2,1)} %get-tuple-element.101), channel_id=1, source_target_pairs={{0,3},{1,0},{3,2},{4,7},{5,4},{6,5},{8,11},{9,8},{11,10},{12,15},{... | collective-permute-start | bytes 3145736 | tf_op jit(solution)/shard_map/cond/branch_3_fun/ppermute | solution.py:143
  29.3 46.1 %collective-permute-start.11 = (bf16[512,1024]{1,0:T(8,128)(2,1)S(1)}, bf16[512,1024]{1,0:T(8,128)(2,1)}, u32[]{:S(2)}, u32[]{:S(2)}) collective-permute-start(bf16[512,1024]{1,0:T(8,128)(2,1)S(1)} %get-tuple-element.102), channel_id=1, source_target_pairs={{1,2},{2,3},{3,0},{4,5},{6,7},{7,4},{9,10},{10,11},{11,8},{12,13},... | collective-permute-start | bytes 3145736 | tf_op jit(solution)/shard_map/cond/branch_3_fun/ppermute | solution.py:143
  75.4 34.9 %copy-start.3 = (bf16[3,256,1024]{2,1,0:T(8,128)(2,1)S(1)}, bf16[3,256,1024]{2,1,0:T(8,128)(2,1)}, u32[]{:S(2)}) copy-start(bf16[3,256,1024]{2,1,0:T(8,128)(2,1)} %get-tuple-element.98.left_ref.refs_1_) | copy-start | bytes 4718596 | tf_op jit(solution)/shard_map/cond
  75.4 34.9 %all-to-all-start.13 = ((bf16[32,16,8,256]{3,2,1,0:T(8,128)(2,1)}), bf16[32,16,8,256]{3,2,1,0:T(8,128)(2,1)}, u32[]{:S(2)}, u32[]{:S(2)}) async-start(bf16[32,16,8,256]{3,2,1,0:T(8,128)(2,1)} %bitcast.40), calls=%async_computation.13 | async-start | bytes 4194304 | tf_op jit(solution)/shard_map/cond/branch_3_fun/all_to_all | solution.py:316
  120.6 32.4 %all-to-all-start.14 = ((bf16[32,16,8,256]{3,2,1,0:T(8,128)(2,1)}), bf16[32,16,8,256]{3,2,1,0:T(8,128)(2,1)S(1)}, u32[]{:S(2)}, u32[]{:S(2)}) async-start(bf16[32,16,8,256]{3,2,1,0:T(8,128)(2,1)} %precondition_slot.9), calls=%async_computation.14 | async-start | bytes 4194304 | tf_op jit(solution)/shard_map/cond/branch_3_fun/all_to_all | solution.py:316
  153.9 66.9 %copy-start.15 = (bf16[128,8,256]{2,1,0:T(8,128)(2,1)S(1)}, bf16[128,8,256]{2,1,0:T(8,128)(2,1)}, u32[]{:S(2)}) copy-start(bf16[128,8,256]{2,1,0:T(8,128)(2,1)} %get-tuple-element.107.parameter_ref) | copy-start | bytes 1572868 | tf_op jit(solution)/shard_map/cond
  220.8 1.1 copy-start.9

commit v7 on v3

--- a/solution.py
+++ b/solution.py
@@ -82,23 +82,14 @@
     return (x + 2 * grid_x - 2 - core) % grid_x
 
 
-def pack_kernel(slot_ref, left_ref, right_ref, *refs):
-    sems, share = refs[-1], left_ref.shape[1]
-    copies = []
-    for at, out in enumerate(refs[:-1]):
-        slot = slot_ref[at]
+def pack_kernel(slot_ref, left_ref, right_ref, out, sems):
+    slot, share = slot_ref[0], left_ref.shape[1]
+    copies = [pltpu.make_async_copy(left_ref.at[slot], out.at[:share], sems.at[grid_x])]
+    for part in range(grid_x):
+        span = pl.ds(part * share, share)
         copies.append(
-            pltpu.make_async_copy(left_ref.at[slot], out.at[:share], sems.at[at * (grid_x + 1)])
+            pltpu.make_async_copy(right_ref.at[slot, span], out.at[share:, span], sems.at[part])
         )
-        for part in range(grid_x):
-            span = pl.ds(part * share, share)
-            copies.append(
-                pltpu.make_async_copy(
-                    right_ref.at[slot, span],
-                    out.at[share:, span],
-                    sems.at[at * (grid_x + 1) + 1 + part],
-                )
-            )
     for copy in copies:
         copy.start()
     for copy in copies:
@@ -107,21 +98,18 @@
 
 def factor_pieces(left_root, right_root, here, core):
     slots, share, order = left_root.shape
-    wanted = jnp.stack(
-        [jnp.minimum(slot_at(here + shift, core), slots - 1) for shift in piece_shifts]
-    )
     hbm_spec = pl.BlockSpec(memory_space=pltpu.HBM)
-    packed = pl.pallas_call(
-        pack_kernel,
-        out_shape=[jax.ShapeDtypeStruct((2 * share, order), left_root.dtype)] * len(piece_shifts),
-        in_specs=[pl.BlockSpec(memory_space=pltpu.SMEM), hbm_spec, hbm_spec],
-        out_specs=[pl.BlockSpec(memory_space=pltpu.VMEM)] * len(piece_shifts),
-        scratch_shapes=[pltpu.SemaphoreType.DMA((len(piece_shifts) * (grid_x + 1),))],
-        compiler_params=pltpu.CompilerParams(vmem_limit_bytes=32 * 1024 * 1024),
-        name="pack_factors",
-    )(wanted, left_root, right_root)
     got = []
-    for shift, piece in zip(piece_shifts, packed):
+    for shift in piece_shifts:
+        piece = pl.pallas_call(
+            pack_kernel,
+            out_shape=jax.ShapeDtypeStruct((2 * share, order), left_root.dtype),
+            in_specs=[pl.BlockSpec(memory_space=pltpu.SMEM), hbm_spec, hbm_spec],
+            out_specs=pl.BlockSpec(memory_space=pltpu.VMEM),
+            scratch_shapes=[pltpu.SemaphoreType.DMA((grid_x + 1,))],
+            compiler_params=pltpu.CompilerParams(vmem_limit_bytes=32 * 1024 * 1024),
+            name="pack_factors",
+        )(jnp.minimum(slot_at(here + shift, core), slots - 1).reshape(1), left_root, right_root)
         pairs = [
             (at * grid_x + src, at * grid_x + (src + shift) % grid_x)
             for at in range(grid_core)
@@ -298,9 +286,9 @@
         return lax.all_to_all(rows, plane_axes, 0, 0, tiled=True)
 
     rows = vmem_call(pick_kernel, [block_at], [gradients], z_rows, "pick_for_z")
-    rows, pieces = lax.optimization_barrier((z_hop(rows), pieces))
     kernel = functools.partial(pick_runs_kernel, (1, plane_cap, grid_z, 1))
-    rows = vmem_call(kernel, [rank_at], [rows], plane_rows, "pick_for_plane")
+    rows = vmem_call(kernel, [rank_at], [z_hop(rows)], plane_rows, "pick_for_plane")
+    rows, pieces = lax.optimization_barrier((rows, pieces))
     rows = plane_hop(rows)
     update = precondition_slot(here, core, rows, left_root, right_root, pieces)
     update = plane_hop(update).reshape((plane_rows,) + chunk)

time: 219 us -> 212 us (0.968)
  waiting for transfers between devices: 92.1 us -> 86.6 us
  Pallas kernels: 19.7 us -> 22.2 us
    ppermute x3, waiting for transfers between devices: 41.1 us -> 5.7 us  [factor_pieces(): got.append(lax.ppermute(piece, ('core', 'x'), pairs))]
    all_to_all x1, waiting for transfers between devices: 0.01 us -> 29.9 us  [z_hop(): lax.all_to_all(rows, 'z', 0, 0, tiled=True).reshape((z_rows,) + chunk)]
    pallas_call x1 -> x3, Pallas kernels: 2.17 us -> 4.59 us  [factor_pieces(): pl.pallas_call(pack_kernel, out_shape=jax.ShapeDtypeStruct((2 * share, or...]
  transfers between devices with their start and end apart: 6 -> 6, of which waited for: 4 -> 4; matrix products, arithmetic and copies ran while one was open for 0% -> 0% of each run, Pallas kernels for 1% -> 3%
where the time goes in v7:
time: 212 us; the launch traced here: 214 us
  waiting for transfers between devices  86.6 us (41%)
  blocking collectives  60.7 us (29%)
  starting transfers between devices  38.6 us (18%)
  Pallas kernels  22.2 us (10%)
  other arithmetic  3.33 us (2%)
    all_to_all x1, blocking collectives, z_hop(): lax.all_to_all(rows, 'z', 0, 0, tiled=True).reshape((z_rows,) + chunk)  60.7 us
    all_to_all x2, waiting for transfers between devices, plane_hop(): return lax.all_to_all(rows, plane_axes, 0, 0, tiled=True)  51 us
    all_to_all x1, waiting for transfers between devices, z_hop(): lax.all_to_all(rows, 'z', 0, 0, tiled=True).reshape((z_rows,) + chunk)  29.9 us
    all_to_all x1, starting transfers between devices, z_hop(): lax.all_to_all(rows, 'z', 0, 0, tiled=True).reshape((z_rows,) + chunk)  15.2 us
    all_to_all x2, starting transfers between devices, plane_hop(): return lax.all_to_all(rows, plane_axes, 0, 0, tiled=True)  14.2 us
    pallas_call x1, Pallas kernels, precondition_slot(): pl.pallas_call(slot_kernel, out_shape=jax.ShapeDtypeStruct(rows.shape, ro...  10.6 us
    ppermute x3, starting transfers between devices, factor_pieces(): got.append(lax.ppermute(piece, ('core', 'x'), pairs))  9.24 us
    pallas_call x5, Pallas kernels, vmem_call(): pl.pallas_call(kernel, out_shape=jax.ShapeDtypeStruct((count,) + arrays[0...  7.01 us
  transfers between devices with their start and end apart: 6, of which 4 were waited for; matrix products, arithmetic and copies ran while one was open for 0% of the time, Pallas kernels for 3%

profile of v7, /device:TPU:6, one launch (start us, length us, event | category | flops | bytes accessed | tf_op | source)
XLA Modules:
  0.0 213.5 jit_solution(3149143552342185228)
XLA Ops:
  0.6 0.7 and_select_fusion.42
  1.4 0.6 fusion.40
  2.7 210.8 %conditional.1 = (bf16[128,8,256]{2,1,0:T(8,128)(2,1)}, bf16[128,8,256]{2,1,0:T(8,128)(2,1)}) conditional(s32[]{:T(128)} %clamp.3, (s32[128]{0:T(128)}, bf16[128,8,256]{2,1,0:T(8,128)(2,1)}, bf16[3,256,1024]{2,1,0:T(8,128)(2,1)}, bf16[3,1024,256]{2,1,0:T(8,128)(2,1)}, bf16[128,8,256]{2,1,0:T(8,128)(2,1)}) %tuple.37, ...), branch_computations={%region_2.7_spmd, %region_7.12_spmd, %region_12.17_spmd, %region_1... | conditional | flops 4295227392 | bytes 61224580 | solution.py:310
  2.8 0.8 compare_select_fusion.10
  4.4 2.4 %pick_for_z.7 = bf16[224,8,256]{2,1,0:T(8,128)(2,1)} custom-call(s32[224]{0:T(256)S(1)} %select_reduce_fusion.3.index_ref, bf16[128,8,256]{2,1,0:T(8,128)(2,1)} %get-tuple-element.70.src_ref), custom_call_target="tpu_custom_call" | custom-call | tf_op jit(solution)/shard_map/cond/branch_1_fun/pick_for_z/pallas_call | solution.py:59
  6.8 15.2 %all-to-all-start.4 = ((bf16[16,14,8,256]{3,2,1,0:T(8,128)(2,1)}), bf16[16,14,8,256]{3,2,1,0:T(8,128)(2,1)S(1)}, u32[]{:S(2)}, u32[]{:S(2)}) async-start(bf16[16,14,8,256]{3,2,1,0:T(8,128)(2,1)} %bitcast.13), calls=%async_computation.4 | async-start | bytes 1835008 | tf_op jit(solution)/shard_map/cond/branch_1_fun/all_to_all | solution.py:282
  22.0 1.2 pack_factors.21
  23.2 1.3 collective-permute-start.3
  24.5 1.2 pack_factors.22
  25.7 3.9 %collective-permute-start.4 = (bf16[512,1024]{1,0:T(8,128)(2,1)S(1)}, bf16[512,1024]{1,0:T(8,128)(2,1)}, u32[]{:S(2)}, u32[]{:S(2)}) collective-permute-start(bf16[512,1024]{1,0:T(8,128)(2,1)S(1)} %pack_factors.22), channel_id=1, source_target_pairs={{0,3},{1,0},{3,2},{4,7},{5,4},{6,5},{8,11},{9,8},{11,10},{12,15},{... | collective-permute-start | bytes 3145736 | tf_op jit(solution)/shard_map/cond/branch_1_fun/ppermute | solution.py:119
  29.6 2.2 %pack_factors.23 = bf16[512,1024]{1,0:T(8,128)(2,1)} custom-call(s32[1]{0:T(128)} %bitcast.17.slot_ref, bf16[3,256,1024]{2,1,0:T(8,128)(2,1)} %get-tuple-element.71.left_ref.refs_1_, bf16[3,1024,256]{2,1,0:T(8,128)(2,1)} %get-tuple-element.72.right_ref.refs_2_), custom_call_target="tpu_custom_call" | custom-call | tf_op jit(solution)/shard_map/cond/branch_1_fun/pack_factors/pallas_call | solution.py:104
  31.8 4.1 %collective-permute-start.5 = (bf16[512,1024]{1,0:T(8,128)(2,1)}, bf16[512,1024]{1,0:T(8,128)(2,1)}, u32[]{:S(2)}, u32[]{:S(2)}) collective-permute-start(bf16[512,1024]{1,0:T(8,128)(2,1)} %pack_factors.23), channel_id=1, source_target_pairs={{1,2},{2,3},{3,0},{4,5},{6,7},{7,4},{9,10},{10,11},{11,8},{12,13},... | collective-permute-start | bytes 3145736 | tf_op jit(solution)/shard_map/cond/branch_1_fun/ppermute | solution.py:119
  36.0 29.9 %all-to-all-done.4 = bf16[16,14,8,256]{3,2,1,0:T(8,128)(2,1)S(1)} async-done(((bf16[16,14,8,256]{3,2,1,0:T(8,128)(2,1)}), bf16[16,14,8,256]{3,2,1,0:T(8,128)(2,1)S(1)}, u32[]{:S(2)}, u32[]{:S(2)}) %all-to-all-start.4) | async-done | bytes 917536 | tf_op jit(solution)/shard_map/cond/branch_1_fun/all_to_all | solution.py:282
  65.9 2.2 %pick_for_plane.7 = bf16[512,8,256]{2,1,0:T(8,128)(2,1)} custom-call(s32[32]{0:T(128)S(1)} %select_reduce_fusion.4.index_ref, bf16[224,8,256]{2,1,0:T(8,128)(2,1)S(1)} %bitcast.84), custom_call_target="tpu_custom_call" | custom-call | tf_op jit(solution)/shard_map/cond/branch_1_fun/pick_for_plane/pallas_call | solution.py:59
  68.1 5.7 %collective-permute-done.4.refs_4_ = bf16[512,1024]{1,0:T(8,128)(2,1)} collective-permute-done((bf16[512,1024]{1,0:T(8,128)(2,1)S(1)}, bf16[512,1024]{1,0:T(8,128)(2,1)}, u32[]{:S(2)}, u32[]{:S(2)}) %collective-permute-start.4) | collective-permute-done | bytes 1048608 | tf_op jit(solution)/shard_map/cond/branch_1_fun/ppermute | solution.py:119
  73.8 7.6 %all-to-all-start.5 = ((bf16[32,16,8,256]{3,2,1,0:T(8,128)(2,1)}), bf16[32,16,8,256]{3,2,1,0:T(8,128)(2,1)}, u32[]{:S(2)}, u32[]{:S(2)}) async-start(bf16[32,16,8,256]{3,2,1,0:T(8,128)(2,1)} %bitcast.18), calls=%async_computation.5 | async-start | bytes 4194304 | tf_op jit(solution)/shard_map/cond/branch_1_fun/all_to_all | solution.py:286
  82.0 25.3 %all-to-all-done.5.refs_0_ = bf16[32,16,8,256]{3,2,1,0:T(8,128)(2,1)} async-done(((bf16[32,16,8,256]{3,2,1,0:T(8,128)(2,1)}), bf16[32,16,8,256]{3,2,1,0:T(8,128)(2,1)}, u32[]{:S(2)}, u32[]{:S(2)}) %all-to-all-start.5) | async-done | bytes 2097184 | tf_op jit(solution)/shard_map/cond/branch_1_fun/all_to_all | solution.py:286
  107.3 10.6 %precondition_slot.7 = bf16[32,16,8,256]{3,2,1,0:T(8,128)(2,1)} custom-call(s32[2]{0:T(128)} %pad_add_fusion.1.here_ref, bf16[32,16,8,256]{3,2,1,0:T(8,128)(2,1)} %all-to-all-done.5.refs_0_, bf16[3,256,1024]{2,1,0:T(8,128)(2,1)S(1)} %copy-done.3, bf16[3,1024,256]{2,1,0:T(8,128)(2,1)S(1)} %copy-done.9, bf16[512,1024]{1,0:T(8,128)(2,1)} %collective-permute-done.3.refs_3_, ...), custom_call_target="tpu_custom_call" | custom-call | flops 4294967296 | bytes 8388608 | tf_op jit(solution)/shard_map/cond/branch_1_fun/precondition_slot/pallas_call | solution.py:227
  117.9 6.5 %all-to-all-start.6 = ((bf16[32,16,8,256]{3,2,1,0:T(8,128)(2,1)}), bf16[32,16,8,256]{3,2,1,0:T(8,128)(2,1)S(1)}, u32[]{:S(2)}, u32[]{:S(2)}) async-start(bf16[32,16,8,256]{3,2,1,0:T(8,128)(2,1)} %precondition_slot.7), calls=%async_computation.6 | async-start | bytes 4194304 | tf_op jit(solution)/shard_map/cond/branch_1_fun/all_to_all | solution.py:286
  124.5 25.7 %all-to-all-done.6 = bf16[32,16,8,256]{3,2,1,0:T(8,128)(2,1)S(1)} async-done(((bf16[32,16,8,256]{3,2,1,0:T(8,128)(2,1)}), bf16[32,16,8,256]{3,2,1,0:T(8,128)(2,1)S(1)}, u32[]{:S(2)}, u32[]{:S(2)}) %all-to-all-start.6) | async-done | bytes 2097184 | tf_op jit(solution)/shard_map/cond/branch_1_fun/all_to_all | solution.py:286
  150.3 0.7 pick_back_for_z.7
  150.9 60.7 %all_to_all.97 = bf16[16,14,8,256]{3,2,1,0:T(8,128)(2,1)S(1)} all-to-all(bf16[16,14,8,256]{3,2,1,0:T(8,128)(2,1)S(1)} %bitcast.85), channel_id=1, replica_groups=mesh['y'=4,'z'=16,'core'=2,'x'=4] {'z'}, dimensions={0} | all-to-all | bytes 1835008 | tf_op jit(solution)/shard_map/cond/branch_1_fun/all_to_all | solution.py:282
  211.7 0.8 pick_step_rows.7.step_ref
  212.5 1.0 step.7
  (23 shorter events, 1.7 us)
Async XLA Ops:
  2.7 19.2 %copy-start.2 = (bf16[3,256,1024]{2,1,0:T(8,128)(2,1)S(1)}, bf16[3,256,1024]{2,1,0:T(8,128)(2,1)}, u32[]{:S(2)}) copy-start(bf16[3,256,1024]{2,1,0:T(8,128)(2,1)} %get-tuple-element.71.left_ref.refs_1_) | copy-start | bytes 4718596 | tf_op jit(solution)/shard_map/cond
  3.7 0.5 copy-start.26
  6.8 59.1 %all-to-all-start.4 = ((bf16[16,14,8,256]{3,2,1,0:T(8,128)(2,1)}), bf16[16,14,8,256]{3,2,1,0:T(8,128)(2,1)S(1)}, u32[]{:S(2)}, u32[]{:S(2)}) async-start(bf16[16,14,8,256]{3,2,1,0:T(8,128)(2,1)} %bitcast.13), calls=%async_computation.4 | async-start | bytes 1835008 | tf_op jit(solution)/shard_map/cond/branch_1_fun/all_to_all | solution.py:282
  23.2 44.9 %collective-permute-start.3 = (bf16[512,1024]{1,0:T(8,128)(2,1)S(1)}, bf16[512,1024]{1,0:T(8,128)(2,1)}, u32[]{:S(2)}, u32[]{:S(2)}) collective-permute-start(bf16[512,1024]{1,0:T(8,128)(2,1)S(1)} %pack_factors.21), channel_id=1, source_target_pairs={{0,2},{1,3},{2,0},{5,7},{6,4},{7,5},{8,10},{9,11},{10,8},{13,15},{... | collective-permute-start | bytes 3145736 | tf_op jit(solution)/shard_map/cond/branch_1_fun/ppermute | solution.py:119
  25.7 48.0 %collective-permute-start.4 = (bf16[512,1024]{1,0:T(8,128)(2,1)S(1)}, bf16[512,1024]{1,0:T(8,128)(2,1)}, u32[]{:S(2)}, u32[]{:S(2)}) collective-permute-start(bf16[512,1024]{1,0:T(8,128)(2,1)S(1)} %pack_factors.22), channel_id=1, source_target_pairs={{0,3},{1,0},{3,2},{4,7},{5,4},{6,5},{8,11},{9,8},{11,10},{12,15},{... | collective-permute-start | bytes 3145736 | tf_op jit(solution)/shard_map/cond/branch_1_fun/ppermute | solution.py:119
  29.6 6.3 %copy-start.27 = (s32[128]{0:T(128)S(1)}, s32[128]{0:T(128)}, u32[]{:S(2)}) copy-start(s32[128]{0:T(128)} %copy-done.26) | copy-start | bytes 1540 | tf_op jit(solution)/shard_map/cond
  31.8 42.0 %collective-permute-start.5 = (bf16[512,1024]{1,0:T(8,128)(2,1)}, bf16[512,1024]{1,0:T(8,128)(2,1)}, u32[]{:S(2)}, u32[]{:S(2)}) collective-permute-start(bf16[512,1024]{1,0:T(8,128)(2,1)} %pack_factors.23), channel_id=1, source_target_pairs={{1,2},{2,3},{3,0},{4,5},{6,7},{7,4},{9,10},{10,11},{11,8},{12,13},... | collective-permute-start | bytes 3145736 | tf_op jit(solution)/shard_map/cond/branch_1_fun/ppermute | solution.py:119
  73.8 33.5 %copy-start.3 = (bf16[3,256,1024]{2,1,0:T(8,128)(2,1)S(1)}, bf16[3,256,1024]{2,1,0:T(8,128)(2,1)}, u32[]{:S(2)}) copy-start(bf16[3,256,1024]{2,1,0:T(8,128)(2,1)} %get-tuple-element.71.left_ref.refs_1_) | copy-start | bytes 4718596 | tf_op jit(solution)/shard_map/cond
  73.8 33.5 %copy-start.9 = (bf16[3,1024,256]{2,1,0:T(8,128)(2,1)S(1)}, bf16[3,1024,256]{2,1,0:T(8,128)(2,1)}, u32[]{:S(2)}) copy-start(bf16[3,1024,256]{2,1,0:T(8,128)(2,1)} %get-tuple-element.72.right_ref.refs_2_) | copy-start | bytes 4718596 | tf_op jit(solution)/shard_map/cond
  73.8 33.5 %all-to-all-start.5 = ((bf16[32,16,8,256]{3,2,1,0:T(8,128)(2,1)}), bf16[32,16,8,256]{3,2,1,0:T(8,128)(2,1)}, u32[]{:S(2)}, u32[]{:S(2)}) async-start(bf16[32,16,8,256]{3,2,1,0:T(8,128)(2,1)} %bitcast.18), calls=%async_computation.5 | async-start | bytes 4194304 | tf_op jit(solution)/shard_map/cond/branch_1_fun/all_to_all | solution.py:286
  117.9 32.4 %all-to-all-start.6 = ((bf16[32,16,8,256]{3,2,1,0:T(8,128)(2,1)}), bf16[32,16,8,256]{3,2,1,0:T(8,128)(2,1)S(1)}, u32[]{:S(2)}, u32[]{:S(2)}) async-start(bf16[32,16,8,256]{3,2,1,0:T(8,128)(2,1)} %precondition_slot.7), calls=%async_computation.6 | async-start | bytes 4194304 | tf_op jit(solution)/shard_map/cond/branch_1_fun/all_to_all | solution.py:286
  150.9 61.5 %copy-start.21 = (bf16[128,8,256]{2,1,0:T(8,128)(2,1)S(1)}, bf16[128,8,256]{2,1,0:T(8,128)(2,1)}, u32[]{:S(2)}) copy-start(bf16[128,8,256]{2,1,0:T(8,128)(2,1)} %get-tuple-element.77.parameter_ref) | copy-start | bytes 1572868 | tf_op jit(solution)/shard_map/cond
  212.5 1.1 copy-start.15

commit v8 on v7

--- a/solution.py
+++ b/solution.py
@@ -27,6 +27,17 @@
         return carry
 
     lax.fori_loop(0, out_ref.shape[0] // pick_run, some, 0)
+
+
+def place_kernel(index_ref, src_ref, out_ref):
+    def some(step, carry):
+        first = step * pick_run
+        rows = [src_ref[first + i] for i in range(pick_run)]
+        for i in range(pick_run):
+            out_ref[index_ref[first + i]] = rows[i]
+        return carry
+
+    lax.fori_loop(0, src_ref.shape[0] // pick_run, some, 0)
 
 
 def pick_runs_kernel(strides, index_ref, src_ref, out_ref):
@@ -271,7 +282,6 @@
     rank = jnp.sum(earlier.astype(jnp.int32), axis=1)
     place_of = plane * plane_cap + rank
     my_z = lax.axis_index("z")
-    block_at = place(ids, place_of, grid_z * plane_cap)
     mine = plane == my_z
     rank_at = place(rank, jnp.where(mine, in_plane, plane_devices), plane_devices)
     holder_at = place(in_plane, jnp.where(mine, rank, plane_cap), plane_cap)
@@ -285,7 +295,7 @@
         rows = rows.reshape((plane_devices, grid_z) + chunk)
         return lax.all_to_all(rows, plane_axes, 0, 0, tiled=True)
 
-    rows = vmem_call(pick_kernel, [block_at], [gradients], z_rows, "pick_for_z")
+    rows = vmem_call(place_kernel, [place_of], [gradients], z_rows, "place_for_z")
     kernel = functools.partial(pick_runs_kernel, (1, plane_cap, grid_z, 1))
     rows = vmem_call(kernel, [rank_at], [z_hop(rows)], plane_rows, "pick_for_plane")
     rows, pieces = lax.optimization_barrier((rows, pieces))

time: 212 us -> 212 us (level); the launches traced: 214 us -> 209 us
  blocking collectives: 60.7 us -> 57.2 us
    all_to_all x1, blocking collectives: 60.7 us -> 57.2 us  [z_hop(): lax.all_to_all(rows, 'z', 0, 0, tiled=True).reshape((z_rows,) + chunk)]
    ppermute x3, waiting for transfers between devices: 5.7 us -> 8.26 us  [factor_pieces(): got.append(lax.ppermute(piece, ('core', 'x'), pairs))]
    all_to_all x1, waiting for transfers between devices: 29.9 us -> 27.3 us  [z_hop(): lax.all_to_all(rows, 'z', 0, 0, tiled=True).reshape((z_rows,) + chunk)]
where the time goes in v8:
time: 212 us; the launch traced here: 209 us
  waiting for transfers between devices  86.5 us (41%)
  blocking collectives  57.2 us (27%)
  starting transfers between devices  38.6 us (18%)
  Pallas kernels  21.9 us (10%)
  other arithmetic  3.25 us (2%)
    all_to_all x1, blocking collectives, z_hop(): lax.all_to_all(rows, 'z', 0, 0, tiled=True).reshape((z_rows,) + chunk)  57.2 us
    all_to_all x2, waiting for transfers between devices, plane_hop(): return lax.all_to_all(rows, plane_axes, 0, 0, tiled=True)  51 us
    all_to_all x1, waiting for transfers between devices, z_hop(): lax.all_to_all(rows, 'z', 0, 0, tiled=True).reshape((z_rows,) + chunk)  27.3 us
    all_to_all x1, starting transfers between devices, z_hop(): lax.all_to_all(rows, 'z', 0, 0, tiled=True).reshape((z_rows,) + chunk)  15.2 us
    all_to_all x2, starting transfers between devices, plane_hop(): return lax.all_to_all(rows, plane_axes, 0, 0, tiled=True)  14.2 us
    pallas_call x1, Pallas kernels, precondition_slot(): pl.pallas_call(slot_kernel, out_shape=jax.ShapeDtypeStruct(rows.shape, ro...  10.5 us
    ppermute x3, starting transfers between devices, factor_pieces(): got.append(lax.ppermute(piece, ('core', 'x'), pairs))  9.24 us
    ppermute x3, waiting for transfers between devices, factor_pieces(): got.append(lax.ppermute(piece, ('core', 'x'), pairs))  8.26 us
  transfers between devices with their start and end apart: 6, of which 4 were waited for; matrix products, arithmetic and copies ran while one was open for 0% of the time, Pallas kernels for 3%

profile of v8, /device:TPU:6, one launch (start us, length us, event | category | flops | bytes accessed | tf_op | source)
XLA Modules:
  0.0 209.0 jit_solution(2465497540356017944)
XLA Ops:
  0.6 0.7 and_select_fusion.42
  1.4 0.6 fusion.40
  2.7 206.3 %conditional.1 = (bf16[128,8,256]{2,1,0:T(8,128)(2,1)}, bf16[128,8,256]{2,1,0:T(8,128)(2,1)}) conditional(s32[]{:T(128)} %clamp.3, (s32[128]{0:T(128)}, bf16[128,8,256]{2,1,0:T(8,128)(2,1)}, bf16[3,256,1024]{2,1,0:T(8,128)(2,1)}, bf16[3,1024,256]{2,1,0:T(8,128)(2,1)}, bf16[128,8,256]{2,1,0:T(8,128)(2,1)}) %tuple.37, ...), branch_computations={%region_2.6_spmd, %region_6.10_spmd, %region_10.14_spmd, %region_1... | conditional | flops 4295080448 | bytes 61223172 | solution.py:320
  2.8 0.8 compare_select_fusion.4
  3.7 2.2 %place_for_z.6 = bf16[208,8,256]{2,1,0:T(8,128)(2,1)} custom-call(s32[128]{0:T(128)S(1)} %get-tuple-element.136.index_ref, bf16[128,8,256]{2,1,0:T(8,128)(2,1)} %get-tuple-element.61.src_ref), custom_call_target="tpu_custom_call" | custom-call | tf_op jit(solution)/shard_map/cond/branch_0_fun/place_for_z/pallas_call | solution.py:70
  5.9 15.2 %all-to-all-start = ((bf16[16,13,8,256]{3,2,1,0:T(8,128)(2,1)}), bf16[16,13,8,256]{3,2,1,0:T(8,128)(2,1)S(1)}, u32[]{:S(2)}, u32[]{:S(2)}) async-start(bf16[16,13,8,256]{3,2,1,0:T(8,128)(2,1)} %bitcast.2), calls=%async_computation | async-start | bytes 1703936 | tf_op jit(solution)/shard_map/cond/branch_0_fun/all_to_all | solution.py:292
  21.2 1.2 pack_factors.18
  22.3 1.3 collective-permute-start
  23.7 1.2 pack_factors.19
  24.9 3.9 %collective-permute-start.1 = (bf16[512,1024]{1,0:T(8,128)(2,1)S(1)}, bf16[512,1024]{1,0:T(8,128)(2,1)}, u32[]{:S(2)}, u32[]{:S(2)}) collective-permute-start(bf16[512,1024]{1,0:T(8,128)(2,1)S(1)} %pack_factors.19), channel_id=1, source_target_pairs={{0,3},{1,0},{3,2},{4,7},{5,4},{6,5},{8,11},{9,8},{11,10},{12,15},{... | collective-permute-start | bytes 3145736 | tf_op jit(solution)/shard_map/cond/branch_0_fun/ppermute | solution.py:130
  28.8 2.2 %pack_factors.20 = bf16[512,1024]{1,0:T(8,128)(2,1)} custom-call(s32[1]{0:T(128)} %bitcast.6.slot_ref, bf16[3,256,1024]{2,1,0:T(8,128)(2,1)} %get-tuple-element.62.left_ref.refs_1_, bf16[3,1024,256]{2,1,0:T(8,128)(2,1)} %get-tuple-element.63.right_ref.refs_2_), custom_call_target="tpu_custom_call" | custom-call | tf_op jit(solution)/shard_map/cond/branch_0_fun/pack_factors/pallas_call | solution.py:115
  31.0 4.1 %collective-permute-start.2 = (bf16[512,1024]{1,0:T(8,128)(2,1)}, bf16[512,1024]{1,0:T(8,128)(2,1)}, u32[]{:S(2)}, u32[]{:S(2)}) collective-permute-start(bf16[512,1024]{1,0:T(8,128)(2,1)} %pack_factors.20), channel_id=1, source_target_pairs={{1,2},{2,3},{3,0},{4,5},{6,7},{7,4},{9,10},{10,11},{11,8},{12,13},... | collective-permute-start | bytes 3145736 | tf_op jit(solution)/shard_map/cond/branch_0_fun/ppermute | solution.py:130
  35.2 27.3 %all-to-all-done = bf16[16,13,8,256]{3,2,1,0:T(8,128)(2,1)S(1)} async-done(((bf16[16,13,8,256]{3,2,1,0:T(8,128)(2,1)}), bf16[16,13,8,256]{3,2,1,0:T(8,128)(2,1)S(1)}, u32[]{:S(2)}, u32[]{:S(2)}) %all-to-all-start) | async-done | bytes 852000 | tf_op jit(solution)/shard_map/cond/branch_0_fun/all_to_all | solution.py:292
  62.5 2.1 %pick_for_plane.6 = bf16[512,8,256]{2,1,0:T(8,128)(2,1)} custom-call(s32[32]{0:T(128)S(1)} %select_reduce_fusion.index_ref, bf16[208,8,256]{2,1,0:T(8,128)(2,1)S(1)} %bitcast.88), custom_call_target="tpu_custom_call" | custom-call | tf_op jit(solution)/shard_map/cond/branch_0_fun/pick_for_plane/pallas_call | solution.py:70
  64.7 8.3 %collective-permute-done.1.refs_4_ = bf16[512,1024]{1,0:T(8,128)(2,1)} collective-permute-done((bf16[512,1024]{1,0:T(8,128)(2,1)S(1)}, bf16[512,1024]{1,0:T(8,128)(2,1)}, u32[]{:S(2)}, u32[]{:S(2)}) %collective-permute-start.1) | collective-permute-done | bytes 1048608 | tf_op jit(solution)/shard_map/cond/branch_0_fun/ppermute | solution.py:130
  72.9 7.6 %all-to-all-start.1 = ((bf16[32,16,8,256]{3,2,1,0:T(8,128)(2,1)}), bf16[32,16,8,256]{3,2,1,0:T(8,128)(2,1)}, u32[]{:S(2)}, u32[]{:S(2)}) async-start(bf16[32,16,8,256]{3,2,1,0:T(8,128)(2,1)} %bitcast.7), calls=%async_computation.1 | async-start | bytes 4194304 | tf_op jit(solution)/shard_map/cond/branch_0_fun/all_to_all | solution.py:296
  81.2 25.3 %all-to-all-done.1.refs_0_ = bf16[32,16,8,256]{3,2,1,0:T(8,128)(2,1)} async-done(((bf16[32,16,8,256]{3,2,1,0:T(8,128)(2,1)}), bf16[32,16,8,256]{3,2,1,0:T(8,128)(2,1)}, u32[]{:S(2)}, u32[]{:S(2)}) %all-to-all-start.1) | async-done | bytes 2097184 | tf_op jit(solution)/shard_map/cond/branch_0_fun/all_to_all | solution.py:296
  106.5 10.5 %precondition_slot.6 = bf16[32,16,8,256]{3,2,1,0:T(8,128)(2,1)} custom-call(s32[2]{0:T(128)} %pad_add_fusion.here_ref, bf16[32,16,8,256]{3,2,1,0:T(8,128)(2,1)} %all-to-all-done.1.refs_0_, bf16[3,256,1024]{2,1,0:T(8,128)(2,1)S(1)} %copy-done.1, bf16[3,1024,256]{2,1,0:T(8,128)(2,1)S(1)} %copy-done.8, bf16[512,1024]{1,0:T(8,128)(2,1)} %collective-permute-done.refs_3_, ...), custom_call_target="tpu_custom_call" | custom-call | flops 4294967296 | bytes 8388608 | tf_op jit(solution)/shard_map/cond/branch_0_fun/precondition_slot/pallas_call | solution.py:238
  117.0 6.5 %all-to-all-start.2 = ((bf16[32,16,8,256]{3,2,1,0:T(8,128)(2,1)}), bf16[32,16,8,256]{3,2,1,0:T(8,128)(2,1)S(1)}, u32[]{:S(2)}, u32[]{:S(2)}) async-start(bf16[32,16,8,256]{3,2,1,0:T(8,128)(2,1)} %precondition_slot.6), calls=%async_computation.2 | async-start | bytes 4194304 | tf_op jit(solution)/shard_map/cond/branch_0_fun/all_to_all | solution.py:296
  123.6 25.7 %all-to-all-done.2 = bf16[32,16,8,256]{3,2,1,0:T(8,128)(2,1)S(1)} async-done(((bf16[32,16,8,256]{3,2,1,0:T(8,128)(2,1)}), bf16[32,16,8,256]{3,2,1,0:T(8,128)(2,1)S(1)}, u32[]{:S(2)}, u32[]{:S(2)}) %all-to-all-start.2) | async-done | bytes 2097184 | tf_op jit(solution)/shard_map/cond/branch_0_fun/all_to_all | solution.py:296
  149.3 0.7 pick_back_for_z.6
  150.0 57.2 %all_to_all.96 = bf16[16,13,8,256]{3,2,1,0:T(8,128)(2,1)S(1)} all-to-all(bf16[16,13,8,256]{3,2,1,0:T(8,128)(2,1)S(1)} %bitcast.89), channel_id=1, replica_groups=mesh['y'=4,'z'=16,'core'=2,'x'=4] {'z'}, dimensions={0} | all-to-all | bytes 1703936 | tf_op jit(solution)/shard_map/cond/branch_0_fun/all_to_all | solution.py:292
  207.2 0.8 pick_step_rows.6.step_ref
  208.0 1.0 step.6
  (18 shorter events, 1.2 us)
Async XLA Ops:
  2.7 18.4 %copy-start = (bf16[3,256,1024]{2,1,0:T(8,128)(2,1)S(1)}, bf16[3,256,1024]{2,1,0:T(8,128)(2,1)}, u32[]{:S(2)}) copy-start(bf16[3,256,1024]{2,1,0:T(8,128)(2,1)} %get-tuple-element.62.left_ref.refs_1_) | copy-start | bytes 4718596 | tf_op jit(solution)/shard_map/cond
  5.9 56.6 %all-to-all-start = ((bf16[16,13,8,256]{3,2,1,0:T(8,128)(2,1)}), bf16[16,13,8,256]{3,2,1,0:T(8,128)(2,1)S(1)}, u32[]{:S(2)}, u32[]{:S(2)}) async-start(bf16[16,13,8,256]{3,2,1,0:T(8,128)(2,1)} %bitcast.2), calls=%async_computation | async-start | bytes 1703936 | tf_op jit(solution)/shard_map/cond/branch_0_fun/all_to_all | solution.py:292
  22.3 42.3 %collective-permute-start = (bf16[512,1024]{1,0:T(8,128)(2,1)S(1)}, bf16[512,1024]{1,0:T(8,128)(2,1)}, u32[]{:S(2)}, u32[]{:S(2)}) collective-permute-start(bf16[512,1024]{1,0:T(8,128)(2,1)S(1)} %pack_factors.18), channel_id=1, source_target_pairs={{0,2},{1,3},{2,0},{5,7},{6,4},{7,5},{8,10},{9,11},{10,8},{13,15},{... | collective-permute-start | bytes 3145736 | tf_op jit(solution)/shard_map/cond/branch_0_fun/ppermute | solution.py:130
  24.9 48.0 %collective-permute-start.1 = (bf16[512,1024]{1,0:T(8,128)(2,1)S(1)}, bf16[512,1024]{1,0:T(8,128)(2,1)}, u32[]{:S(2)}, u32[]{:S(2)}) collective-permute-start(bf16[512,1024]{1,0:T(8,128)(2,1)S(1)} %pack_factors.19), channel_id=1, source_target_pairs={{0,3},{1,0},{3,2},{4,7},{5,4},{6,5},{8,11},{9,8},{11,10},{12,15},{... | collective-permute-start | bytes 3145736 | tf_op jit(solution)/shard_map/cond/branch_0_fun/ppermute | solution.py:130
  31.0 41.9 %collective-permute-start.2 = (bf16[512,1024]{1,0:T(8,128)(2,1)}, bf16[512,1024]{1,0:T(8,128)(2,1)}, u32[]{:S(2)}, u32[]{:S(2)}) collective-permute-start(bf16[512,1024]{1,0:T(8,128)(2,1)} %pack_factors.20), channel_id=1, source_target_pairs={{1,2},{2,3},{3,0},{4,5},{6,7},{7,4},{9,10},{10,11},{11,8},{12,13},... | collective-permute-start | bytes 3145736 | tf_op jit(solution)/shard_map/cond/branch_0_fun/ppermute | solution.py:130
  72.9 33.5 %copy-start.1 = (bf16[3,256,1024]{2,1,0:T(8,128)(2,1)S(1)}, bf16[3,256,1024]{2,1,0:T(8,128)(2,1)}, u32[]{:S(2)}) copy-start(bf16[3,256,1024]{2,1,0:T(8,128)(2,1)} %get-tuple-element.62.left_ref.refs_1_) | copy-start | bytes 4718596 | tf_op jit(solution)/shard_map/cond
  72.9 33.5 %copy-start.8 = (bf16[3,1024,256]{2,1,0:T(8,128)(2,1)S(1)}, bf16[3,1024,256]{2,1,0:T(8,128)(2,1)}, u32[]{:S(2)}) copy-start(bf16[3,1024,256]{2,1,0:T(8,128)(2,1)} %get-tuple-element.63.right_ref.refs_2_) | copy-start | bytes 4718596 | tf_op jit(solution)/shard_map/cond
  72.9 33.5 %all-to-all-start.1 = ((bf16[32,16,8,256]{3,2,1,0:T(8,128)(2,1)}), bf16[32,16,8,256]{3,2,1,0:T(8,128)(2,1)}, u32[]{:S(2)}, u32[]{:S(2)}) async-start(bf16[32,16,8,256]{3,2,1,0:T(8,128)(2,1)} %bitcast.7), calls=%async_computation.1 | async-start | bytes 4194304 | tf_op jit(solution)/shard_map/cond/branch_0_fun/all_to_all | solution.py:296
  117.0 32.4 %all-to-all-start.2 = ((bf16[32,16,8,256]{3,2,1,0:T(8,128)(2,1)}), bf16[32,16,8,256]{3,2,1,0:T(8,128)(2,1)S(1)}, u32[]{:S(2)}, u32[]{:S(2)}) async-start(bf16[32,16,8,256]{3,2,1,0:T(8,128)(2,1)} %precondition_slot.6), calls=%async_computation.2 | async-start | bytes 4194304 | tf_op jit(solution)/shard_map/cond/branch_0_fun/all_to_all | solution.py:296
  150.0 58.0 %copy-start.20 = (bf16[128,8,256]{2,1,0:T(8,128)(2,1)S(1)}, bf16[128,8,256]{2,1,0:T(8,128)(2,1)}, u32[]{:S(2)}) copy-start(bf16[128,8,256]{2,1,0:T(8,128)(2,1)} %get-tuple-element.68.parameter_ref) | copy-start | bytes 1572868 | tf_op jit(solution)/shard_map/cond
  208.0 1.1 copy-start.14
